TPU v7x, 128 devices: a whole 4x4x4 slice. The times are simulated.
128 devices in a mesh: grp: 16 (over y_lo, x, core), tile: 8 (over y_hi, z).
Axes of the slice: x: 4, y: 4 (y_hi: 2, y_lo: 2; y = y_hi * 2 + y_lo), z: 4, core: 2. Of those that a mesh axis runs over, the one named last changes fastest.
Arguments:
- coeff: bfloat16 [64, 256, 4096], P('grp', None, 'tile'), may hold values from -0.09375 to 0.09375
- energy: float32 [64, 4096], P('grp', 'tile'), may hold values from 1 to 3
- ranks: int32 [64, 64], replicated, may hold values from 32 to 256, as said below
- assign: int32 [4096], P(('grp', 'tile')), may hold values from 0 to 4095, each once
- screen: bfloat16 [4096, 256, 256], P(('grp', 'tile')), may hold values from -0.375 to 0.375
- initial: float32 [64, 8, 4096], P('grp', None, 'tile'), may hold values from -6 to 6
Outputs:
- rayleigh: float32 [2, 8, 8], replicated
- basis: float32 [64, 8, 4096], P('grp', None, 'tile')
- residual: float32 [64, 8, 4096], P('grp', None, 'tile')
Inputs may be any that keep to these rules, and one draw needn't show every extreme that they name: ranks is symmetric and its diagonal equals 256. `assign`: every pair index appears exactly once.
All inputs are finite; a program needn't handle non-finite values.
Results may differ from a plain program's by a relative error of at most 0.0075.
Values may be sent and summed in bfloat16 or wider, within the bound.
A program may use at most 64 MiB of HBM per device.

v0:
```python
import jax
import jax.numpy as jnp
from jax import lax
from jax.sharding import PartitionSpec as P

ITERS = 2


def inner_sum(left, right):
    return jnp.einsum("knp,kmp->nm", left, right, precision=lax.Precision.HIGHEST)


def combine_rows(weights, block):
    return jnp.einsum("mn,kmp->knp", weights, block, precision=lax.Precision.HIGHEST)


def orthonormal(block, count):
    gram = lax.psum(inner_sum(block, block), ("grp", "tile")) / count
    lower = jnp.linalg.cholesky(gram)
    vectors = block.shape[1]
    inverse = lax.linalg.triangular_solve(
        lower, jnp.eye(vectors, dtype=jnp.float32), left_side=True, lower=True
    )
    return combine_rows(inverse.T, block)


def apply_kernel(block, coeff, energy, ranks, assign, screen):
    local_k, vectors, _ = block.shape
    levels_count = coeff.shape[1]
    block_b = block.astype(jnp.bfloat16)
    dens_part = jnp.einsum("knp,kgp->kng", block_b, coeff, preferred_element_type=jnp.float32)
    dens_local = lax.psum(dens_part, "tile")
    dens_b = lax.all_gather(dens_local.astype(jnp.bfloat16), "grp", axis=0, tiled=True)
    total_k = dens_b.shape[0]
    task_row = assign // total_k
    task_col = assign % total_k
    task_rank = ranks[task_row, task_col]
    levels = jnp.arange(levels_count, dtype=jnp.int32)
    keep = (levels[None, :] < task_rank[:, None]).astype(jnp.float32)
    task_dens = dens_b[task_col] * keep.astype(jnp.bfloat16)[:, None, :]
    task_out = jnp.einsum("tnh,tgh->tng", task_dens, screen, preferred_element_type=jnp.float32)
    task_out = task_out * keep[:, None, :]
    onehot = (task_row[None, :] == jnp.arange(total_k, dtype=jnp.int32)[:, None]).astype(
        jnp.float32
    )
    partial_rows = jnp.dot(
        onehot,
        task_out.reshape(task_out.shape[0], vectors * levels_count),
        precision=lax.Precision.HIGHEST,
    )
    summed_tile = lax.psum(partial_rows, "tile")
    owned = lax.psum_scatter(summed_tile, "grp", scatter_dimension=0, tiled=True)
    rows_b = owned.reshape(local_k, vectors, levels_count).astype(jnp.bfloat16)
    coupled = jnp.einsum("kng,kgp->knp", rows_b, coeff, preferred_element_type=jnp.float32)
    return energy[:, None, :] * block + coupled


def per_device(coeff, energy, ranks, assign, screen, initial):
    count = initial.shape[0] * lax.axis_size("grp") * initial.shape[2] * lax.axis_size("tile")
    basis = orthonormal(initial, count)
    collected = []
    residual = initial
    for step in range(ITERS):
        sigma = apply_kernel(basis, coeff, energy, ranks, assign, screen)
        scaled_energy = energy[:, None, :]
        projected = lax.psum(inner_sum(basis, sigma), ("grp", "tile")) / count
        residual = sigma - combine_rows(projected, basis)
        precond = residual / scaled_energy
        correlation = lax.psum(inner_sum(basis, precond), ("grp", "tile")) / count
        collected.append(projected)
        direction = precond - combine_rows(correlation, basis)
        basis = orthonormal(direction, count)
    return (jnp.stack(collected), basis, residual)


def solution(mesh):
    placed = (
        P("grp", None, "tile"),
        P("grp", "tile"),
        P(),
        P(("grp", "tile")),
        P(("grp", "tile"), None, None),
        P("grp", None, "tile"),
    )
    return jax.shard_map(
        per_device,
        mesh=mesh,
        in_specs=placed,
        out_specs=(P(), P("grp", None, "tile"), P("grp", None, "tile")),
        check_vma=False,
    )
```

profile of v0, /device:TPU:1, one launch (start us, length us, event | category | flops | bytes accessed | tf_op | source)
XLA Modules:
  0.0 915.2 jit_solution(15024559700116579816)
XLA Ops:
  7.2 1.1 convolution_bitcast_fusion.16
  8.4 68.7 %psum.77 = f32[8,8]{0,1:T(8,128)S(1)} all-reduce(f32[8,8]{0,1:T(8,128)S(1)} %convolution_bitcast_fusion.16), channel_id=1, replica_groups=mesh['grp'=16,'tile'=8] {'grp','tile'}, use_global_device_ids=true, to_apply=%region_0.0 | all-reduce | flops 64 | bytes 512 | tf_op jit(solution)/shard_map/psum | solution.py:18
  80.0 1.0 convolution_bitcast_fusion.6
  81.4 32.2 %psum.78 = bf16[4,8,256]{2,1,0:T(8,128)(2,1)S(1)} all-reduce(f32[4,8,256]{2,1,0:T(8,128)S(1)} %fusion.11), channel_id=1, replica_groups=mesh['grp'=16,'tile'=8] {'tile'}, use_global_device_ids=true, to_apply=%region_3.6 | all-reduce | flops 8192 | bytes 49152 | tf_op jit(solution)/shard_map/psum | solution.py:32
  113.7 25.3 %all_gather.6 = bf16[64,8,256]{2,1,0:T(8,128)(2,1)S(1)} all-gather(bf16[4,8,256]{2,1,0:T(8,128)(2,1)S(1)} %psum.78), channel_id=1, replica_groups=mesh['grp'=16,'tile'=8] {'grp'}, dimensions={0}, use_global_device_ids=true | all-gather | bytes 278528 | tf_op jit(solution)/shard_map/all_gather | solution.py:33
  139.6 1.5 gather_fusion.1
  141.8 3.4 convolution_multiply_fusion.1
  145.2 1.2 fusion.14
  147.7 111.5 %all-reduce.5.cloned.1.call-done = f32[64,2048]{1,0:T(8,128)} async-done(((f32[64,2048]{1,0:T(8,128)}), f32[64,2048]{1,0:T(8,128)}) %all-reduce.5.cloned.1.call-update) | async-done | bytes 524304
  259.2 0.8 constant_dynamic-slice_fusion.1
  260.1 34.5 %psum.88 = bf16[4,2048]{1,0:T(4,128)(2,1)S(1)} all-reduce(f32[4,2048]{1,0:T(4,128)S(1)} %constant_dynamic-slice_fusion.1), channel_id=1, replica_groups=mesh['grp'=16,'tile'=8] {'tile'}, use_global_device_ids=true, to_apply=%region_4.7 | all-reduce | flops 8192 | bytes 49152 | tf_op jit(solution)/shard_map/psum | solution.py:51
  295.0 69.6 %psum.80 = f32[8,8]{0,1:T(8,128)S(1)} all-reduce(f32[8,8]{0,1:T(8,128)S(1)} %convolution_bitcast_fusion.14), channel_id=1, replica_groups=mesh['grp'=16,'tile'=8] {'grp','tile'}, use_global_device_ids=true, to_apply=%region_6.9 | all-reduce | flops 64 | bytes 512 | tf_op jit(solution)/shard_map/psum | solution.py:66
  365.0 62.5 %psum.81 = f32[8,8]{0,1:T(8,128)S(1)} all-reduce(f32[8,8]{0,1:T(8,128)S(1)} %convolution_bitcast_fusion.13), channel_id=1, replica_groups=mesh['grp'=16,'tile'=8] {'grp','tile'}, use_global_device_ids=true, to_apply=%region_7.10 | all-reduce | flops 64 | bytes 512 | tf_op jit(solution)/shard_map/psum | solution.py:69
  427.9 64.0 %psum.82 = f32[8,8]{0,1:T(8,128)S(1)} all-reduce(f32[8,8]{0,1:T(8,128)S(1)} %convolution_bitcast_fusion.12), channel_id=1, replica_groups=mesh['grp'=16,'tile'=8] {'grp','tile'}, use_global_device_ids=true, to_apply=%region_8.11 | all-reduce | flops 64 | bytes 512 | tf_op jit(solution)/shard_map/psum | solution.py:18
  495.5 31.2 %psum.83 = bf16[4,8,256]{2,1,0:T(8,128)(2,1)S(1)} all-reduce(f32[4,8,256]{2,1,0:T(8,128)S(1)} %fusion.9), channel_id=1, replica_groups=mesh['grp'=16,'tile'=8] {'tile'}, use_global_device_ids=true, to_apply=%region_9.12 | all-reduce | flops 8192 | bytes 49152 | tf_op jit(solution)/shard_map/psum | solution.py:32
  526.7 25.6 %all_gather.7 = bf16[64,8,256]{2,1,0:T(8,128)(2,1)S(1)} all-gather(bf16[4,8,256]{2,1,0:T(8,128)(2,1)S(1)} %psum.83), channel_id=1, replica_groups=mesh['grp'=16,'tile'=8] {'grp'}, dimensions={0}, use_global_device_ids=true | all-gather | bytes 278528 | tf_op jit(solution)/shard_map/all_gather | solution.py:33
  552.9 3.4 convolution_multiply_fusion
  556.4 1.2 fusion.13
  557.7 113.3 %all-reduce.7.cloned.1.call-done = f32[64,2048]{1,0:T(8,128)} async-done(((f32[64,2048]{1,0:T(8,128)}), f32[64,2048]{1,0:T(8,128)}) %all-reduce.7.cloned.1.call-update) | async-done | bytes 524304
  670.9 0.8 constant_dynamic-slice_fusion
  671.8 34.5 %psum.89 = bf16[4,2048]{1,0:T(4,128)(2,1)S(1)} all-reduce(f32[4,2048]{1,0:T(4,128)S(1)} %constant_dynamic-slice_fusion), channel_id=1, replica_groups=mesh['grp'=16,'tile'=8] {'tile'}, use_global_device_ids=true, to_apply=%region_10.13 | all-reduce | flops 8192 | bytes 49152 | tf_op jit(solution)/shard_map/psum | solution.py:51
  706.7 69.6 %psum.85 = f32[8,8]{0,1:T(8,128)S(1)} all-reduce(f32[8,8]{0,1:T(8,128)S(1)} %convolution_bitcast_fusion.10), channel_id=1, replica_groups=mesh['grp'=16,'tile'=8] {'grp','tile'}, use_global_device_ids=true, to_apply=%region_12.15 | all-reduce | flops 64 | bytes 512 | tf_op jit(solution)/shard_map/psum | solution.py:66
  776.7 62.7 %psum.86 = f32[8,8]{0,1:T(8,128)S(1)} all-reduce(f32[8,8]{0,1:T(8,128)S(1)} %convolution_bitcast_fusion.9), channel_id=1, replica_groups=mesh['grp'=16,'tile'=8] {'grp','tile'}, use_global_device_ids=true, to_apply=%region_13.16 | all-reduce | flops 64 | bytes 512 | tf_op jit(solution)/shard_map/psum | solution.py:69
  839.8 64.0 %psum.87 = f32[8,8]{0,1:T(8,128)S(1)} all-reduce(f32[8,8]{0,1:T(8,128)S(1)} %convolution_bitcast_fusion.8), channel_id=1, replica_groups=mesh['grp'=16,'tile'=8] {'grp','tile'}, use_global_device_ids=true, to_apply=%region_14.17 | all-reduce | flops 64 | bytes 512 | tf_op jit(solution)/shard_map/psum | solution.py:18
  (68 shorter events, 16.6 us)
Async XLA Ops:
  7.2 73.9 %copy-start = (bf16[4,256,512]{2,1,0:T(8,128)(2,1)S(1)}, bf16[4,256,512]{2,1,0:T(8,128)(2,1)}, u32[]{:S(2)}) copy-start(bf16[4,256,512]{2,1,0:T(8,128)(2,1)} %param.9) | copy-start | bytes 3145732
  7.2 252.1 %all-reduce.5.cloned.1.call-start = ((), (), s32[]{:S(2)}) async-start(), calls=%async_computation | async-start | bytes 1048576
  81.0 65.4 %copy-start.3 = (u32[128]{0:T(128)S(1)}, u32[128]{0:T(128)}, u32[]{:S(2)}) copy-start(u32[128]{0:T(128)} %constant.93) | copy-start | bytes 1540
  81.4 213.2 %copy-start.2 = (f32[4,512]{1,0:T(4,128)S(1)}, f32[4,512]{1,0:T(4,128)}, u32[]{:S(2)}) copy-start(f32[4,512]{1,0:T(4,128)} %param.10) | copy-start | bytes 24580
  146.4 524.5 %all-reduce.7.cloned.1.call-start = ((), (), s32[]{:S(2)}) async-start(), calls=%async_computation.1 | async-start | bytes 1048576
  776.5 131.8 %copy-start.1 = (f32[4,8,512]{2,1,0:T(8,128)}, f32[4,8,512]{2,1,0:T(8,128)S(1)}, u32[]{:S(2)}) copy-start(f32[4,8,512]{2,1,0:T(8,128)S(1)} %fusion.1) | copy-start | bytes 196612
Sparse Core Ops, SparseCore 0:
  146.6 112.6 all-reduce.4
  557.7 113.1 all-reduce.6
where the time goes:
time: 917 us; the launch traced here: 915 us
  blocking collectives  644 us (70%)
  waiting for transfers between devices  225 us (25%)
  matrix products  16.1 us (2%)
  between operations  14.9 us (2%)
  other arithmetic  9.39 us (1%)
    unnamed x4, waiting for transfers between devices  225 us
    psum x3, blocking collectives, orthonormal(): gram = lax.psum(inner_sum(block, block), ('grp', 'tile')) / count  197 us
    psum x2, blocking collectives, per_device(): projected = lax.psum(inner_sum(basis, sigma), ('grp', 'tile')) / count  139 us
    psum x2, blocking collectives, per_device(): correlation = lax.psum(inner_sum(basis, precond), ('grp', 'tile')) / count  125 us
    psum x2, blocking collectives, apply_kernel(): summed_tile = lax.psum(partial_rows, 'tile')  69 us
    psum x2, blocking collectives, apply_kernel(): dens_local = lax.psum(dens_part, 'tile')  63.4 us
    all_gather x2, blocking collectives, apply_kernel(): lax.all_gather(dens_local.astype(jnp.bfloat16), 'grp', axis=0, tiled=True)  50.9 us
  transfers between devices with their start and end apart: 2, of which 2 were waited for; matrix products, arithmetic and copies ran while one was open for 0% of the time, Pallas kernels for 0%

commit v1 on v0

v1 whole, which is shorter than its diff:
```python
import functools

import jax
import jax.numpy as jnp
from jax import lax
from jax.experimental import pallas as pl
from jax.experimental.pallas import tpu as pltpu
from jax.sharding import PartitionSpec as P

ITERS = 2
NV = 8
GRP, TILE, CHIPS, CORES = 16, 8, 8, 2
LK = 4
ROWS = LK * NV
ALL = GRP * ROWS
LEV = 256
TASKS = 32
SPAN = 128
F32, BF16 = jnp.float32, jnp.bfloat16
HIGHEST = lax.Precision.HIGHEST
MESH = pl.DeviceIdType.MESH
CHIP_STEPS = ((1, 2), (0, 2), (1, 1), (1, 3), (0, 1), (0, 3), (1, 0))
TILE_STEPS = ((1, 2), (1, 1), (1, 3), (1, 0), (0, 2), (0, 1), (0, 3))


def dot(a, b, nt=False, precision=None):
    return lax.dot_general(
        a, b, (((1,), (1 if nt else 0,)), ((), ())),
        precision=precision, preferred_element_type=F32,
    )


def split(a):
    high = a.astype(BF16)
    return high, (a - high.astype(F32)).astype(BF16)


def iota(shape, dim):
    return lax.broadcasted_iota(jnp.int32, shape, dim)


def block_mask(rows, cols):
    return (iota((rows, cols), 0) // NV) == (iota((rows, cols), 1) // NV)


def fold(part):
    for step in (8, 16, 32, 64):
        part = part + pltpu.roll(part, step, 1)
    return part


def sum_groups(a):
    total = a[0:NV]
    for i in range(1, a.shape[0] // NV):
        total = total + a[i * NV:(i + 1) * NV]
    return total


def spread(small, mask):
    return jnp.where(mask, jnp.concatenate([small] * (SPAN // NV), axis=0), 0.0)


def inverse_factor(gram):
    sub, lane = iota((NV, SPAN), 0), iota((NV, SPAN), 1) % NV
    right = (sub == lane).astype(F32)
    pivots = jnp.ones((NV, SPAN), F32)
    for j in range(NV):
        row, other = gram[j:j + 1, :], right[j:j + 1, :]
        pivot = jnp.broadcast_to(row[:, j:j + 1], (NV, SPAN))
        pivots = jnp.where(sub == j, pivot, pivots)
        factor = jnp.broadcast_to(gram[:, j:j + 1], (NV, SPAN)) / pivot
        factor = jnp.where(sub > j, factor, 0.0)
        gram = gram - factor * row
        right = right - factor * other
    return right * lax.rsqrt(pivots)


def body(
    count, assign_ref, ranks_ref, coeff_hbm, screen_hbm, energy_ref, x_ref,
    ray_ref, basis_ref, res_ref,
    coeff, screen, d1, d2, dens, term, part, e8, pick, keep,
    r1s, r1, a1s, a1, r2s, r2, a2, r3, a3, f1, f2,
    load_sem, send, recv,
):
    g, t = lax.axis_index("grp"), lax.axis_index("tile")
    core, chip = lax.rem(g, CORES), lax.div(g, CORES)
    y_lo, x = lax.div(chip, 4), lax.rem(chip, 4)
    y_hi, z = lax.div(t, 4), lax.rem(t, 4)
    sibling = (chip * CORES + (1 - core), t)
    chip_ids = [lax.rem(y_lo + a, 2) * 4 + lax.rem(x + b, 4) for a, b in CHIP_STEPS]
    chips = [(c * CORES + core, t) for c in chip_ids]
    tiles = [(g, lax.rem(y_hi + a, 2) * 4 + lax.rem(z + b, 4)) for a, b in TILE_STEPS]

    half_rows = ALL // 2
    barrier = pltpu.get_barrier_semaphore()
    peers = [sibling, *chips, *tiles]
    for peer in peers:
        pl.semaphore_signal(barrier, inc=1, device_id=peer, device_id_type=MESH)
    load_coeff = pltpu.make_async_copy(coeff_hbm, coeff, load_sem.at[0])
    load_screen = pltpu.make_async_copy(screen_hbm, screen, load_sem.at[1])
    load_coeff.start()
    load_screen.start()

    used = []

    def push(src, dst, index, device):
        pltpu.make_async_remote_copy(
            src_ref=src, dst_ref=dst, send_sem=send.at[index], recv_sem=recv.at[index],
            device_id=device, device_id_type=MESH,
        ).start()

    def await_bytes(ref, sems, index):
        pltpu.make_async_copy(ref, ref, sems.at[index]).wait()

    def gather(buf, mine, devices, index):
        for device in devices:
            push(buf.at[mine], buf.at[mine], index, device)
        await_bytes(buf.at[pl.ds(0, len(devices))], recv, index)
        used.append((buf.at[pl.ds(0, len(devices))], index))

    mask = block_mask(SPAN, SPAN)
    mask_gram = ((iota((2 * ROWS, 2 * ROWS), 0) % ROWS) // NV) == (
        (iota((2 * ROWS, 2 * ROWS), 1) % ROWS) // NV
    )
    section = iota((NV, SPAN), 1) // ROWS

    def grams(left, right):
        full = jnp.where(mask_gram, dot(left, right, nt=True, precision=HIGHEST), 0.0)
        return jnp.concatenate([sum_groups(full[:ROWS]), sum_groups(full[ROWS:])], axis=1)

    def project(block):
        high, low = split(block)
        out = []
        for k in range(LK):
            rows = slice(k * NV, (k + 1) * NV)
            both = jnp.concatenate([block[rows], low[rows].astype(F32)], axis=0).astype(BF16)
            got = dot(both, coeff[k], nt=True)
            out.append(got[:NV] + got[NV:])
        return jnp.concatenate(out, axis=0)

    def section_of(total, which):
        return fold(jnp.where(section == which, total, 0.0)) * (1.0 / count)

    energy = jnp.concatenate(
        [jnp.broadcast_to(energy_ref[k:k + 1, :], (NV, energy_ref.shape[1])) for k in range(LK)],
        axis=0,
    )
    block = x_ref[...]
    scaled = energy * block
    zeros = jnp.zeros_like(block)
    load_coeff.wait()
    payload = project(block)
    sums = grams(jnp.concatenate([block, scaled], 0), jnp.concatenate([zeros, block], 0))

    def place(k):
        return ((k >> 2) & 1) * half_rows + (k >> 3) * ROWS + (k & 3) * NV

    lane_task = iota((1, half_rows), 1) // NV
    target = jnp.zeros((1, half_rows), jnp.int32)
    pairs = []
    for i in range(TASKS):
        pair = assign_ref[i]
        target = jnp.where(lane_task == i, place(pair >> 6), target)
        pairs.append(jnp.full((NV, SPAN), pair, jnp.int32))
    target = target + iota((1, half_rows), 1) % NV
    e8[...] = (iota((ALL, half_rows), 0) == target).astype(F32).astype(BF16)
    pairs = jnp.concatenate(pairs, axis=0)
    task_row, task_col = pairs >> 6, pairs & 63
    lane = iota((half_rows, SPAN), 1)
    source_row = place(task_col) + iota((half_rows, SPAN), 0) % NV
    for j in range(ALL // SPAN):
        pick[:, j * SPAN:(j + 1) * SPAN] = (lane + j * SPAN == source_row).astype(F32).astype(BF16)
    chosen = dot((lane[:, :GRP * LK] == task_row[:, :GRP * LK]).astype(F32).astype(BF16),
                 ranks_ref[...].astype(F32).astype(BF16))
    chosen = jnp.where(lane[:, :GRP * LK] == task_col[:, :GRP * LK], chosen, 0.0)
    rank = jnp.sum(chosen, axis=1, keepdims=True)
    keep[...] = (iota((half_rows, LEV), 1).astype(F32) < rank).astype(F32)

    pl.semaphore_wait(barrier, len(peers))

    basis = None
    own_energy = None
    for step in range(ITERS):
        d1[step, t, 0:ROWS, :] = payload
        d1[step, t, ROWS:, :] = jnp.concatenate([sums, jnp.zeros_like(sums)], axis=1)
        gather(d1.at[step], t, tiles, 10 * step + 0)
        total = d1[step, 0]
        for i in range(1, TILE):
            total = total + d1[step, i]
        d2[step, core, chip] = total
        gather(d2.at[step, core], chip, chips, 10 * step + 1)
        push(d2.at[step, core], d2.at[step, core], 10 * step + 2, sibling)
        await_bytes(d2.at[step, 0], recv, 10 * step + 2)
        used.append((d2.at[step, 0], 10 * step + 2))

        total = jnp.zeros((NV, SPAN), F32)
        for i in range(CHIPS):
            for c in range(CORES):
                total = total + d2[step, c, i, ROWS:, 0:SPAN]
        pv, pp, rv, rp = [section_of(total, i) for i in range(4)]
        pv_spread = spread(pv, mask)
        if step == 0:
            gram = pp
        else:
            gram = pp - dot(pv, pv_spread, nt=True, precision=HIGHEST)
        inverse = inverse_factor(gram)
        inverse_spread = spread(inverse, mask)
        inv_high, inv_low = split(inverse_spread)
        pv_high, pv_low = split(pv_spread)

        def apply(high, low, rows):
            rows_high, rows_low = split(rows)
            return (
                dot(jnp.concatenate([high, high], axis=1), jnp.concatenate([rows_high, rows_low], axis=0))
                + dot(low, rows_high)
            )

        for j in range(ALL // SPAN):
            raw = jnp.concatenate(
                [d2[step, j // 2, (j % 2) * 4 + i, 0:ROWS, :] for i in range(4)], axis=0
            )
            if step:
                raw = raw - apply(pv_high, pv_low, dens[step - 1, j * SPAN:(j + 1) * SPAN, :])
            dens[step, j * SPAN:(j + 1) * SPAN, :] = apply(inv_high, inv_low, raw)

        if step:
            block = block - dot(pv_spread[:ROWS, :ROWS], basis, precision=HIGHEST)
            crossed = dot(rv, pv_spread, nt=True, precision=HIGHEST)
            crossed_t = dot(pv, spread(rv, mask), nt=True, precision=HIGHEST)
            inner = dot(pv, spread(own_energy, mask), precision=HIGHEST)
            rp = rp - crossed - crossed_t + dot(inner, pv_spread, nt=True, precision=HIGHEST)
        basis = dot(inverse_spread[:ROWS, :ROWS], block, precision=HIGHEST)
        half = dot(inverse, spread(rp, mask), precision=HIGHEST)
        own_energy = dot(half, inverse_spread, nt=True, precision=HIGHEST)

        if step == 0:
            load_screen.wait()
        chosen = dot(pick[...], dens[step].astype(BF16)) * keep[...]
        for i in range(TASKS):
            rows = slice(i * NV, (i + 1) * NV)
            term[rows, :] = dot(chosen[rows].astype(BF16), screen[i], nt=True)
        term_high, term_low = split(term[...] * keep[...])
        part[...] = dot(e8[...], term_high) + dot(e8[...], term_low)
        coupled = jnp.zeros((SPAN, SPAN), F32)
        for j in range(ALL // SPAN):
            rows = slice(j * SPAN, (j + 1) * SPAN)
            coupled = coupled + dot(part[rows, :].astype(BF16), dens[step, rows, :].astype(BF16), nt=True)
        coupled = sum_groups(jnp.where(mask, coupled, 0.0))

        theirs = pl.ds(pl.multiple_of((1 - core) * half_rows, half_rows), half_rows)
        r1s[step] = part[theirs, :].astype(BF16)
        a1s[step] = coupled
        push(r1s.at[step], r1.at[step], 10 * step + 3, sibling)
        push(a1s.at[step], a1.at[step], 10 * step + 4, sibling)
        mine = part[pl.ds(pl.multiple_of(core * half_rows, half_rows), half_rows), :]
        await_bytes(r1.at[step], recv, 10 * step + 3)
        await_bytes(a1.at[step], recv, 10 * step + 4)
        used.append((r1.at[step], 10 * step + 3))
        used.append((a1.at[step], 10 * step + 4))
        summed = (mine + r1[step].astype(F32)).astype(BF16)
        for i in range(CHIPS):
            r2s[step, i] = summed[i * ROWS:(i + 1) * ROWS]
        a2[step, chip] = coupled + a1[step]
        for c, device in zip(chip_ids, chips):
            push(r2s.at[step, c], r2.at[step, chip], 10 * step + 5, device)
        gather_index = 10 * step + 6
        r2[step, chip] = r2s[step, chip]
        gather(a2.at[step], chip, chips, gather_index)
        await_bytes(r2.at[step, pl.ds(0, CHIPS - 1)], recv, 10 * step + 5)
        used.append((r2.at[step, pl.ds(0, CHIPS - 1)], 10 * step + 5))
        rows_sum = r2[step, 0].astype(F32)
        a_sum = a2[step, 0]
        for i in range(1, CHIPS):
            rows_sum = rows_sum + r2[step, i].astype(F32)
            a_sum = a_sum + a2[step, i]
        r3[step, t] = rows_sum.astype(BF16)
        a3[step, t] = a_sum
        for device in tiles:
            push(r3.at[step, t], r3.at[step, t], 10 * step + 7, device)
        gather(a3.at[step], t, tiles, 10 * step + 8)
        await_bytes(r3.at[step, pl.ds(0, TILE - 1)], recv, 10 * step + 7)
        used.append((r3.at[step, pl.ds(0, TILE - 1)], 10 * step + 7))
        rows_sum = r3[step, 0].astype(F32)
        a_sum = a3[step, 0]
        for i in range(1, TILE):
            rows_sum = rows_sum + r3[step, i].astype(F32)
            a_sum = a_sum + a3[step, i]

        ray_t = fold(a_sum) * (1.0 / count) + own_energy
        eye = (iota((NV, SPAN), 0) == iota((NV, SPAN), 1)).astype(F32)
        first = jnp.where(iota((NV, SPAN), 1) < NV, ray_t, 0.0)
        ray_ref[step] = dot(eye, first, nt=True, precision=HIGHEST)
        rows_b = rows_sum.astype(BF16)
        sigma = energy * basis + jnp.concatenate(
            [dot(rows_b[k * NV:(k + 1) * NV], coeff[k]) for k in range(LK)], axis=0
        )
        residual = sigma - dot(spread(ray_t, mask)[:ROWS, :ROWS], basis, precision=HIGHEST)
        block = residual / energy
        sums = grams(
            jnp.concatenate([block, residual], 0), jnp.concatenate([basis, block], 0)
        )
        if step + 1 < ITERS:
            payload = project(block)

    res_ref[...] = residual
    f1[t] = sums
    gather(f1, t, tiles, 10 * ITERS)
    total = f1[0]
    for i in range(1, TILE):
        total = total + f1[i]
    f2[core, chip] = total
    gather(f2.at[core], chip, chips, 10 * ITERS + 1)
    push(f2.at[core], f2.at[core], 10 * ITERS + 2, sibling)
    await_bytes(f2.at[0], recv, 10 * ITERS + 2)
    used.append((f2.at[0], 10 * ITERS + 2))
    total = jnp.zeros((NV, SPAN), F32)
    for i in range(CHIPS):
        for c in range(CORES):
            total = total + f2[c, i]
    pv, pp = section_of(total, 0), section_of(total, 1)
    pv_spread = spread(pv, mask)
    gram = pp - dot(pv, pv_spread, nt=True, precision=HIGHEST)
    inverse_spread = spread(inverse_factor(gram), mask)
    block = block - dot(pv_spread[:ROWS, :ROWS], basis, precision=HIGHEST)
    basis_ref[...] = dot(inverse_spread[:ROWS, :ROWS], block, precision=HIGHEST)

    for ref, index in used:
        await_bytes(ref, send, index)


def per_device(coeff, energy, ranks, assign, screen, initial):
    width = initial.shape[2]
    count = initial.shape[0] * GRP * width * TILE
    vmem = pl.BlockSpec(memory_space=pltpu.VMEM)
    smem = pl.BlockSpec(memory_space=pltpu.SMEM)
    anywhere = pl.BlockSpec(memory_space=pl.ANY)
    phases = 10 * ITERS + 3
    ray, basis, residual = pl.pallas_call(
        functools.partial(body, count),
        out_shape=[
            jax.ShapeDtypeStruct((ITERS, NV, NV), F32),
            jax.ShapeDtypeStruct((ROWS, width), F32),
            jax.ShapeDtypeStruct((ROWS, width), F32),
        ],
        in_specs=[smem, vmem, anywhere, anywhere, vmem, vmem],
        out_specs=[vmem, vmem, vmem],
        scratch_shapes=[
            pltpu.VMEM(coeff.shape, BF16),
            pltpu.VMEM(screen.shape, BF16),
            pltpu.VMEM((ITERS, TILE, ROWS + NV, LEV), F32),
            pltpu.VMEM((ITERS, CORES, CHIPS, ROWS + NV, LEV), F32),
            pltpu.VMEM((ITERS, ALL, LEV), F32),
            pltpu.VMEM((ALL // 2, LEV), F32),
            pltpu.VMEM((ALL, LEV), F32),
            pltpu.VMEM((ALL, ALL // 2), BF16),
            pltpu.VMEM((ALL // 2, ALL), BF16),
            pltpu.VMEM((ALL // 2, LEV), F32),
            pltpu.VMEM((ITERS, ALL // 2, LEV), BF16),
            pltpu.VMEM((ITERS, ALL // 2, LEV), BF16),
            pltpu.VMEM((ITERS, NV, SPAN), F32),
            pltpu.VMEM((ITERS, NV, SPAN), F32),
            pltpu.VMEM((ITERS, CHIPS, ROWS, LEV), BF16),
            pltpu.VMEM((ITERS, CHIPS, ROWS, LEV), BF16),
            pltpu.VMEM((ITERS, CHIPS, NV, SPAN), F32),
            pltpu.VMEM((ITERS, TILE, ROWS, LEV), BF16),
            pltpu.VMEM((ITERS, TILE, NV, SPAN), F32),
            pltpu.VMEM((TILE, NV, SPAN), F32),
            pltpu.VMEM((CORES, CHIPS, NV, SPAN), F32),
            pltpu.SemaphoreType.DMA((2,)),
            pltpu.SemaphoreType.DMA((phases,)),
            pltpu.SemaphoreType.DMA((phases,)),
        ],
        compiler_params=pltpu.CompilerParams(
            collective_id=0, has_side_effects=True, vmem_limit_bytes=48 * 2**20
        ),
        name="davidson",
    )(assign, ranks, coeff, screen, energy, initial.reshape(ROWS, width))
    return ray, basis.reshape(initial.shape), residual.reshape(initial.shape)


def solution(mesh):
    placed = (
        P("grp", None, "tile"),
        P("grp", "tile"),
        P(),
        P(("grp", "tile")),
        P(("grp", "tile"), None, None),
        P("grp", None, "tile"),
    )
    return jax.shard_map(
        per_device,
        mesh=mesh,
        in_specs=placed,
        out_specs=(P(), P("grp", None, "tile"), P("grp", None, "tile")),
        check_vma=False,
    )
```

time: 917 us -> 87.1 us (0.09)
  blocking collectives: 644 us -> 0 us
  waiting for transfers between devices: 225 us -> 0 us
  Pallas kernels: 0 us -> 77.9 us
  matrix products: 16.1 us -> 0 us
  between operations: 14.9 us -> 0.65 us
  other arithmetic: 9.39 us -> 0 us
    psum x11 -> x0, blocking collectives: 594 us -> none  [the longest x3 197 us: orthonormal(): gram = lax.psum(inner_sum(block, block), ('grp', 'tile')) / count]
    unnamed x4 -> x0, waiting for transfers between devices: 225 us -> none
    pallas_call x0 -> x1, Pallas kernels: none -> 77.9 us  [per_device(): pl.pallas_call(functools.partial(body, count), out_shape=[jax.ShapeDtypeS...]
    all_gather x2 -> x0, blocking collectives: 50.9 us -> none  [apply_kernel(): lax.all_gather(dens_local.astype(jnp.bfloat16), 'grp', axis=0, tiled=True)]
    dot_general x22 -> x0, matrix products: 15.5 us -> none  [the longest x2 6.74 us: apply_kernel(): jnp.einsum('tnh,tgh->tng', task_dens, screen, preferred_element_type=jnp....]
  transfers between devices with their start and end apart: 2 -> 0, of which waited for: 2 -> 0; matrix products, arithmetic and copies ran while one was open for 0% -> 0% of each run, Pallas kernels for 0% -> 0%
where the time goes in v1:
time: 87.1 us; the launch traced here: 86.7 us
  Pallas kernels  77.9 us (89%)
  local copies, waits for them, and re-layouts  8.21 us (9%)
    pallas_call x1, Pallas kernels, per_device(): pl.pallas_call(functools.partial(body, count), out_shape=[jax.ShapeDtypeS...  77.9 us
    unnamed x15, local copies, waits for them, and re-layouts  8.21 us

profile of v1, /device:TPU:1, one launch (start us, length us, event | category | flops | bytes accessed | tf_op | source)
XLA Modules:
  0.0 86.7 jit_solution(5948101429125795122)
XLA Ops:
  0.6 0.0 copy-start
  0.6 2.2 %copy-done = bf16[32,256,256]{2,1,0:T(8,128)(2,1)S(1)} copy-done((bf16[32,256,256]{2,1,0:T(8,128)(2,1)S(1)}, bf16[32,256,256]{2,1,0:T(8,128)(2,1)}, u32[]{:S(2)}) %copy-start) | copy-done | bytes 4194328
  2.8 0.0 copy-start.1
  2.8 1.2 %copy-done.1 = bf16[4,256,512]{2,1,0:T(8,128)(2,1)S(1)} copy-done((bf16[4,256,512]{2,1,0:T(8,128)(2,1)S(1)}, bf16[4,256,512]{2,1,0:T(8,128)(2,1)}, u32[]{:S(2)}) %copy-start.1) | copy-done | bytes 1048600
  4.0 0.0 copy-start.2
  4.0 0.8 copy-done.2
  4.9 0.0 copy-start.3
  4.9 0.8 copy-done.3
  5.6 0.0 copy-start.4
  5.6 0.7 copy-done.4
  6.3 0.0 copy-start.5
  6.3 0.7 copy-done.5
  7.0 77.9 %davidson.1 = (f32[2,8,8]{2,1,0:T(8,128)S(1)}, f32[32,512]{1,0:T(8,128)S(1)}, f32[32,512]{1,0:T(8,128)S(1)}) custom-call(s32[32]{0:T(128)S(1)} %copy-done.5, s32[64,64]{1,0:T(8,128)S(1)} %copy-done.3, bf16[4,256,512]{2,1,0:T(8,128)(2,1)S(1)} %copy-done.1, bf16[32,256,256]{2,1,0:T(8,128)(2,1)S(1)} %copy-done, f32[4,512]{1,0:T(4,128)S(1)} %copy-done.4, ...), custom_call_target="tpu_custom_call" | custom-call | tf_op jit(solution)/shard_map/davidson/pallas_call | solution.py:338
  84.9 0.6 copy.12
  85.5 0.6 copy.13
  86.1 0.6 copy.14
Async XLA Ops:
  0.6 2.2 %copy-start = (bf16[32,256,256]{2,1,0:T(8,128)(2,1)S(1)}, bf16[32,256,256]{2,1,0:T(8,128)(2,1)}, u32[]{:S(2)}) copy-start(bf16[32,256,256]{2,1,0:T(8,128)(2,1)} %screen_hbm.1) | copy-start | bytes 12582916
  2.8 1.2 %copy-start.1 = (bf16[4,256,512]{2,1,0:T(8,128)(2,1)S(1)}, bf16[4,256,512]{2,1,0:T(8,128)(2,1)}, u32[]{:S(2)}) copy-start(bf16[4,256,512]{2,1,0:T(8,128)(2,1)} %coeff_hbm.1) | copy-start | bytes 3145732
  4.0 0.8 copy-start.2
  4.9 0.8 copy-start.3
  5.6 0.7 copy-start.4
  6.3 0.7 copy-start.5

commit v2 on v1

--- a/solution.py
+++ b/solution.py
@@ -76,11 +76,11 @@
 
 
 def body(
-    count, assign_ref, ranks_ref, coeff_hbm, screen_hbm, energy_ref, x_ref,
+    count, assign_hbm, ranks_hbm, coeff_hbm, screen_hbm, energy_hbm, x_hbm,
     ray_ref, basis_ref, res_ref,
     coeff, screen, d1, d2, dens, term, part, e8, pick, keep,
     r1s, r1, a1s, a1, r2s, r2, a2, r3, a3, f1, f2,
-    load_sem, send, recv,
+    assign_ref, ranks_ref, energy_ref, x_ref, load_sem, send, recv,
 ):
     g, t = lax.axis_index("grp"), lax.axis_index("tile")
     core, chip = lax.rem(g, CORES), lax.div(g, CORES)
@@ -96,10 +96,15 @@
     peers = [sibling, *chips, *tiles]
     for peer in peers:
         pl.semaphore_signal(barrier, inc=1, device_id=peer, device_id_type=MESH)
-    load_coeff = pltpu.make_async_copy(coeff_hbm, coeff, load_sem.at[0])
-    load_screen = pltpu.make_async_copy(screen_hbm, screen, load_sem.at[1])
-    load_coeff.start()
-    load_screen.start()
+    loads = [
+        pltpu.make_async_copy(src, dst, load_sem.at[i])
+        for i, (src, dst) in enumerate((
+            (x_hbm, x_ref), (coeff_hbm, coeff), (energy_hbm, energy_ref),
+            (assign_hbm, assign_ref), (ranks_hbm, ranks_ref), (screen_hbm, screen),
+        ))
+    ]
+    for load in loads:
+        load.start()
 
     used = []
 
@@ -141,6 +146,8 @@
     def section_of(total, which):
         return fold(jnp.where(section == which, total, 0.0)) * (1.0 / count)
 
+    for load in loads[:3]:
+        load.wait()
     energy = jnp.concatenate(
         [jnp.broadcast_to(energy_ref[k:k + 1, :], (NV, energy_ref.shape[1])) for k in range(LK)],
         axis=0,
@@ -148,9 +155,11 @@
     block = x_ref[...]
     scaled = energy * block
     zeros = jnp.zeros_like(block)
-    load_coeff.wait()
     payload = project(block)
     sums = grams(jnp.concatenate([block, scaled], 0), jnp.concatenate([zeros, block], 0))
+
+    for load in loads[3:5]:
+        load.wait()
 
     def place(k):
         return ((k >> 2) & 1) * half_rows + (k >> 3) * ROWS + (k & 3) * NV
@@ -234,7 +243,7 @@
         own_energy = dot(half, inverse_spread, nt=True, precision=HIGHEST)
 
         if step == 0:
-            load_screen.wait()
+            loads[5].wait()
         chosen = dot(pick[...], dens[step].astype(BF16)) * keep[...]
         for i in range(TASKS):
             rows = slice(i * NV, (i + 1) * NV)
@@ -332,8 +341,7 @@
     width = initial.shape[2]
     count = initial.shape[0] * GRP * width * TILE
     vmem = pl.BlockSpec(memory_space=pltpu.VMEM)
-    smem = pl.BlockSpec(memory_space=pltpu.SMEM)
-    anywhere = pl.BlockSpec(memory_space=pl.ANY)
+    hbm = pl.BlockSpec(memory_space=pltpu.HBM)
     phases = 10 * ITERS + 3
     ray, basis, residual = pl.pallas_call(
         functools.partial(body, count),
@@ -342,7 +350,7 @@
             jax.ShapeDtypeStruct((ROWS, width), F32),
             jax.ShapeDtypeStruct((ROWS, width), F32),
         ],
-        in_specs=[smem, vmem, anywhere, anywhere, vmem, vmem],
+        in_specs=[hbm] * 6,
         out_specs=[vmem, vmem, vmem],
         scratch_shapes=[
             pltpu.VMEM(coeff.shape, BF16),
@@ -366,12 +374,16 @@
             pltpu.VMEM((ITERS, TILE, NV, SPAN), F32),
             pltpu.VMEM((TILE, NV, SPAN), F32),
             pltpu.VMEM((CORES, CHIPS, NV, SPAN), F32),
-            pltpu.SemaphoreType.DMA((2,)),
+            pltpu.SMEM(assign.shape, jnp.int32),
+            pltpu.VMEM(ranks.shape, jnp.int32),
+            pltpu.VMEM(energy.shape, F32),
+            pltpu.VMEM((ROWS, width), F32),
+            pltpu.SemaphoreType.DMA((6,)),
             pltpu.SemaphoreType.DMA((phases,)),
             pltpu.SemaphoreType.DMA((phases,)),
         ],
         compiler_params=pltpu.CompilerParams(
-            collective_id=0, has_side_effects=True, vmem_limit_bytes=48 * 2**20
+            collective_id=0, has_side_effects=True, vmem_limit_bytes=54 * 2**20
         ),
         name="davidson",
     )(assign, ranks, coeff, screen, energy, initial.reshape(ROWS, width))

time: 87.1 us -> 83.3 us (0.956)
  local copies, waits for them, and re-layouts: 8.21 us -> 4.24 us
    unnamed x15 -> x3, local copies, waits for them, and re-layouts: 8.21 us -> 4.24 us
where the time goes in v2:
time: 83.3 us; the launch traced here: 83.1 us
  Pallas kernels  78.2 us (94%)
  local copies, waits for them, and re-layouts  4.24 us (5%)
    pallas_call x1, Pallas kernels, per_device(): pl.pallas_call(functools.partial(body, count), out_shape=[jax.ShapeDtypeS...  78.2 us
    unnamed x3, local copies, waits for them, and re-layouts  4.24 us

profile of v2, /device:TPU:1, one launch (start us, length us, event | category | flops | bytes accessed | tf_op | source)
XLA Modules:
  0.0 83.1 jit_solution(11625057520667020076)
XLA Ops:
  0.6 78.2 %davidson.1 = (f32[2,8,8]{2,1,0:T(8,128)}, f32[32,512]{1,0:T(8,128)}, f32[32,512]{1,0:T(8,128)}) custom-call(s32[32]{0:T(128)} %assign_hbm.1, s32[64,64]{1,0:T(8,128)} %ranks_hbm.1, bf16[4,256,512]{2,1,0:T(8,128)(2,1)} %coeff_hbm.1, bf16[32,256,256]{2,1,0:T(8,128)(2,1)} %screen_hbm.1, f32[4,512]{1,0:T(4,128)} %energy_hbm.1, f32[32,512]{1,0:T(8,128)} %bitcast.3), custom_call_target="tpu_custom_call" | custom-call | tf_op jit(solution)/shard_map/davidson/pallas_call | solution.py:346
  78.8 1.3 %copy.12 = f32[2,8,8]{2,1,0:T(8,128)} copy(f32[2,8,8]{2,1,0:T(8,128)} %get-tuple-element.12) | data formatting | bytes 1024
  80.1 1.5 %copy.13 = f32[4,8,512]{2,1,0:T(8,128)} copy(f32[4,8,512]{2,1,0:T(8,128)} %bitcast.5) | data formatting | bytes 131072
  81.6 1.5 %copy.14 = f32[4,8,512]{2,1,0:T(8,128)} copy(f32[4,8,512]{2,1,0:T(8,128)} %bitcast.4) | data formatting | bytes 131072

commit v3 on v2

v3 whole, which is shorter than its diff:
```python
import functools

import jax
import jax.numpy as jnp
from jax import lax
from jax.experimental import pallas as pl
from jax.experimental.pallas import tpu as pltpu
from jax.sharding import PartitionSpec as P

ITERS = 2
NV = 8
GRP, TILE, CHIPS, CORES = 16, 8, 8, 2
LK = 4
ROWS = LK * NV
ALL = GRP * ROWS
LEV = 256
TASKS = 32
SEMS = 64
SPAN = 128
F32, BF16 = jnp.float32, jnp.bfloat16
HIGHEST = lax.Precision.HIGHEST
MESH = pl.DeviceIdType.MESH
CHIP_STEPS = ((1, 2), (0, 2), (1, 1), (1, 3), (0, 1), (0, 3), (1, 0))
TILE_STEPS = ((1, 2), (1, 1), (1, 3), (1, 0), (0, 2), (0, 1), (0, 3))


def dot(a, b, nt=False, precision=None):
    return lax.dot_general(
        a, b, (((1,), (1 if nt else 0,)), ((), ())),
        precision=precision, preferred_element_type=F32,
    )


def split(a):
    high = a.astype(BF16)
    return high, (a - high.astype(F32)).astype(BF16)


def iota(shape, dim):
    return lax.broadcasted_iota(jnp.int32, shape, dim)


def block_mask(rows, cols):
    return (iota((rows, cols), 0) // NV) == (iota((rows, cols), 1) // NV)


def fold(part):
    for step in (8, 16, 32, 64):
        part = part + pltpu.roll(part, step, 1)
    return part


def sum_groups(a):
    total = a[0:NV]
    for i in range(1, a.shape[0] // NV):
        total = total + a[i * NV:(i + 1) * NV]
    return total


def spread(small, mask):
    return jnp.where(mask, jnp.concatenate([small] * (SPAN // NV), axis=0), 0.0)


def inverse_factor(gram):
    sub, lane = iota((NV, SPAN), 0), iota((NV, SPAN), 1) % NV
    right = (sub == lane).astype(F32)
    pivots = jnp.ones((NV, SPAN), F32)
    for j in range(NV):
        row, other = gram[j:j + 1, :], right[j:j + 1, :]
        pivot = jnp.broadcast_to(row[:, j:j + 1], (NV, SPAN))
        pivots = jnp.where(sub == j, pivot, pivots)
        factor = jnp.broadcast_to(gram[:, j:j + 1], (NV, SPAN)) / pivot
        factor = jnp.where(sub > j, factor, 0.0)
        gram = gram - factor * row
        right = right - factor * other
    return right * lax.rsqrt(pivots)


def body(
    count, assign_hbm, ranks_hbm, coeff_hbm, screen_hbm, energy_hbm, x_hbm,
    ray_ref, basis_ref, res_ref,
    coeff, screen, g1, g2, d1, d2, dens, dens_b, term, e8, pick, keep,
    r1s, r1, a1s, a1, r2s, r2, a2, r3, a3, f1, f2,
    assign_ref, ranks_ref, energy_ref, x_ref, load_sem, send, recv,
):
    g, t = lax.axis_index("grp"), lax.axis_index("tile")
    core, chip = lax.rem(g, CORES), lax.div(g, CORES)
    y_lo, x = lax.div(chip, 4), lax.rem(chip, 4)
    y_hi, z = lax.div(t, 4), lax.rem(t, 4)
    sibling = (chip * CORES + (1 - core), t)
    to_ids = [lax.rem(y_lo + a, 2) * 4 + lax.rem(x + b, 4) for a, b in CHIP_STEPS]
    from_ids = [lax.rem(y_lo + 2 - a, 2) * 4 + lax.rem(x + 4 - b, 4) for a, b in CHIP_STEPS]
    chips = [(c * CORES + core, t) for c in to_ids]
    tiles = [(g, lax.rem(y_hi + a, 2) * 4 + lax.rem(z + b, 4)) for a, b in TILE_STEPS]

    half_rows = ALL // 2
    barrier = pltpu.get_barrier_semaphore()
    peers = [*tiles, *chips, sibling]
    for peer in peers:
        pl.semaphore_signal(barrier, inc=1, device_id=peer, device_id_type=MESH)
    loads = [
        pltpu.make_async_copy(src, dst, load_sem.at[i])
        for i, (src, dst) in enumerate((
            (x_hbm, x_ref), (energy_hbm, energy_ref), (coeff_hbm, coeff),
            (assign_hbm, assign_ref), (ranks_hbm, ranks_ref), (screen_hbm, screen),
        ))
    ]
    for load in loads:
        load.start()

    used = []
    numbers = iter(range(SEMS))

    def push(src, dst, index, device):
        pltpu.make_async_remote_copy(
            src_ref=src, dst_ref=dst, send_sem=send.at[index], recv_sem=recv.at[index],
            device_id=device, device_id_type=MESH,
        ).start()

    def await_bytes(ref, sems, index):
        pltpu.make_async_copy(ref, ref, sems.at[index]).wait()

    def offer(buf, mine, devices):
        index = next(numbers)
        for device in devices:
            push(buf.at[mine], buf.at[mine], index, device)
        size = buf.at[pl.ds(0, len(devices))]
        used.append((size, index))
        return lambda: await_bytes(size, recv, index)

    def hand(src, dst):
        index = next(numbers)
        push(src, dst, index, sibling)
        used.append((dst, index))
        return lambda: await_bytes(dst, recv, index)

    def add_up(buf, n):
        total = buf[0].astype(F32)
        for i in range(1, n):
            total = total + buf[i].astype(F32)
        return total

    mask = block_mask(SPAN, SPAN)
    mask_gram = ((iota((2 * ROWS, 2 * ROWS), 0) % ROWS) // NV) == (
        (iota((2 * ROWS, 2 * ROWS), 1) % ROWS) // NV
    )
    section = iota((NV, SPAN), 1) // ROWS

    def grams(left, right):
        full = jnp.where(mask_gram, dot(left, right, nt=True, precision=HIGHEST), 0.0)
        return jnp.concatenate([sum_groups(full[:ROWS]), sum_groups(full[ROWS:])], axis=1)

    def project(block):
        low = block - block.astype(BF16).astype(F32)
        out = []
        for k in range(LK):
            rows = slice(k * NV, (k + 1) * NV)
            both = jnp.concatenate([block[rows], low[rows]], axis=0).astype(BF16)
            got = dot(both, coeff[k], nt=True)
            out.append(got[:NV] + got[NV:])
        return jnp.concatenate(out, axis=0)

    def section_of(total, which):
        return fold(jnp.where(section == which, total, 0.0)) * (1.0 / count)

    def place(k):
        return ((k >> 2) & 1) * half_rows + (k >> 3) * ROWS + (k & 3) * NV

    def one_hots():
        for load in loads[3:5]:
            load.wait()
        lane_task = iota((1, half_rows), 1) // NV
        target = jnp.zeros((1, half_rows), jnp.int32)
        pairs = []
        for i in range(TASKS):
            pair = assign_ref[i]
            target = jnp.where(lane_task == i, place(pair >> 6), target)
            pairs.append(jnp.full((NV, SPAN), pair, jnp.int32))
        target = target + iota((1, half_rows), 1) % NV
        e8[...] = (iota((ALL, half_rows), 0) == target).astype(F32).astype(BF16)
        pairs = jnp.concatenate(pairs, axis=0)
        task_row, task_col = pairs >> 6, pairs & 63
        lane = iota((half_rows, SPAN), 1)
        source_row = place(task_col) + iota((half_rows, SPAN), 0) % NV
        for j in range(ALL // SPAN):
            pick[:, j * SPAN:(j + 1) * SPAN] = (
                (lane + j * SPAN == source_row).astype(F32).astype(BF16)
            )
        k_points = GRP * LK
        chosen = dot((lane[:, :k_points] == task_row[:, :k_points]).astype(F32).astype(BF16),
                     ranks_ref[...].astype(F32).astype(BF16))
        chosen = jnp.where(lane[:, :k_points] == task_col[:, :k_points], chosen, 0.0)
        rank = jnp.sum(chosen, axis=1, keepdims=True)
        keep[...] = (iota((half_rows, LEV), 1).astype(F32) < rank).astype(F32)

    def apply(high, low, rows):
        rows_high, rows_low = split(rows)
        return (
            dot(jnp.concatenate([high, high], axis=1), jnp.concatenate([rows_high, rows_low], axis=0))
            + dot(low, rows_high)
        )

    for load in loads[:2]:
        load.wait()
    energy = jnp.concatenate(
        [jnp.broadcast_to(energy_ref[k:k + 1, :], (NV, energy_ref.shape[1])) for k in range(LK)],
        axis=0,
    )
    block = x_ref[...]
    zeros = jnp.zeros_like(block)
    sums = grams(jnp.concatenate([block, energy * block], 0), jnp.concatenate([zeros, block], 0))
    loads[2].wait()
    payload = project(block)
    pl.semaphore_wait(barrier, len(peers))

    basis = None
    own_energy = None
    residual = None
    mine = pl.ds(pl.multiple_of(core * half_rows, half_rows), half_rows)
    theirs = pl.ds(pl.multiple_of((1 - core) * half_rows, half_rows), half_rows)
    for step in range(ITERS):
        g1[step, t] = sums
        wait_g1 = offer(g1.at[step], t, tiles)
        if step:
            payload = project(block)
        d1[step, t] = payload
        wait_d1 = offer(d1.at[step], t, tiles)
        if step == 0:
            one_hots()
        wait_g1()
        g2[step, core, chip] = add_up(g1.at[step], TILE)
        wait_g2 = offer(g2.at[step, core], chip, chips)
        wait_d1()
        d2[step, core, chip] = add_up(d1.at[step], TILE)
        mine_now = d2.at[step, core, chip]
        arrivals = [next(numbers) for _ in chips]
        for index, device in zip(arrivals, chips):
            push(mine_now, mine_now, index, device)
            used.append((mine_now, index))
        pass_on = next(numbers)
        push(mine_now, mine_now, pass_on, sibling)
        wait_g2()
        hand(g2.at[step, core], g2.at[step, core])()

        total = jnp.zeros((NV, SPAN), F32)
        for i in range(CHIPS):
            for c in range(CORES):
                total = total + g2[step, c, i]
        pv, pp, rv, rp = [section_of(total, i) for i in range(4)]
        pv_spread = spread(pv, mask)
        gram = pp
        if step:
            gram = pp - dot(pv, pv_spread, nt=True, precision=HIGHEST)
        inverse = inverse_factor(gram)
        inverse_spread = spread(inverse, mask)
        inv_high, inv_low = split(inverse_spread)
        pv_high, pv_low = split(pv_spread)

        for index, source in reversed(list(zip(arrivals, from_ids))):
            landed = d2.at[step, core, source]
            await_bytes(landed, recv, index)
            push(landed, landed, pass_on, sibling)
        whole = d2.at[step, 0]
        used.append((whole, pass_on))
        await_bytes(whole, recv, pass_on)
        for j in range(ALL // SPAN):
            rows = slice(j * SPAN, (j + 1) * SPAN)
            raw = jnp.concatenate(
                [d2[step, j // 2, (j % 2) * 4 + i] for i in range(4)], axis=0
            )
            if step:
                raw = raw - apply(pv_high, pv_low, dens[rows, :])
            raw = apply(inv_high, inv_low, raw)
            dens_b[rows, :] = raw.astype(BF16)
            if step + 1 < ITERS:
                dens[rows, :] = raw

        if step == 0:
            loads[5].wait()
        chosen = dot(pick[...], dens_b[...]) * keep[...]
        for i in range(TASKS):
            rows = slice(i * NV, (i + 1) * NV)
            term[rows, :] = dot(chosen[rows].astype(BF16), screen[i], nt=True)
        term_high, term_low = split(term[...] * keep[...])

        r1s[step] = (dot(e8[theirs, :], term_high) + dot(e8[theirs, :], term_low)).astype(BF16)
        wait_r1 = hand(r1s.at[step], r1.at[step])
        own = dot(e8[mine, :], term_high) + dot(e8[mine, :], term_low)
        own_b = own.astype(BF16)
        coupled = jnp.zeros((SPAN, SPAN), F32)
        for j in range(half_rows // SPAN):
            rows = slice(j * SPAN, (j + 1) * SPAN)
            coupled = coupled + dot(r1s[step, rows, :], dens_b[theirs, :][rows], nt=True)
            coupled = coupled + dot(own_b[rows], dens_b[mine, :][rows], nt=True)
        coupled = sum_groups(jnp.where(mask, coupled, 0.0))
        a1s[step] = coupled
        wait_a1 = hand(a1s.at[step], a1.at[step])
        wait_r1()
        summed = (own + r1[step].astype(F32)).astype(BF16)
        for i in range(CHIPS):
            r2s[step, i] = summed[i * ROWS:(i + 1) * ROWS]
        r2_index = next(numbers)
        for c, device in zip(to_ids, chips):
            push(r2s.at[step, c], r2.at[step, chip], r2_index, device)
        r2[step, chip] = r2s[step, chip]
        r2_size = r2.at[step, pl.ds(0, CHIPS - 1)]
        used.append((r2_size, r2_index))
        wait_a1()
        a2[step, chip] = coupled + a1[step]
        wait_a2 = offer(a2.at[step], chip, chips)

        if step:
            block = block - dot(pv_spread[:ROWS, :ROWS], basis, precision=HIGHEST)
            crossed = dot(rv, pv_spread, nt=True, precision=HIGHEST)
            crossed_t = dot(pv, spread(rv, mask), nt=True, precision=HIGHEST)
            inner = dot(pv, spread(own_energy, mask), precision=HIGHEST)
            rp = rp - crossed - crossed_t + dot(inner, pv_spread, nt=True, precision=HIGHEST)
        basis = dot(inverse_spread[:ROWS, :ROWS], block, precision=HIGHEST)
        half = dot(inverse, spread(rp, mask), precision=HIGHEST)
        own_energy = dot(half, inverse_spread, nt=True, precision=HIGHEST)

        await_bytes(r2_size, recv, r2_index)
        r3[step, t] = add_up(r2.at[step], CHIPS).astype(BF16)
        wait_r3 = offer(r3.at[step], t, tiles)
        wait_a2()
        a3[step, t] = add_up(a2.at[step], CHIPS)
        wait_a3 = offer(a3.at[step], t, tiles)
        wait_r3()
        rows_b = add_up(r3.at[step], TILE).astype(BF16)
        sigma = energy * basis + jnp.concatenate(
            [dot(rows_b[k * NV:(k + 1) * NV], coeff[k]) for k in range(LK)], axis=0
        )
        wait_a3()
        ray_t = fold(add_up(a3.at[step], TILE)) * (1.0 / count) + own_energy
        residual = sigma - dot(spread(ray_t, mask)[:ROWS, :ROWS], basis, precision=HIGHEST)
        block = residual / energy
        sums = grams(
            jnp.concatenate([block, residual], 0), jnp.concatenate([basis, block], 0)
        )
        eye = (iota((NV, SPAN), 0) == iota((NV, SPAN), 1)).astype(F32)
        first = jnp.where(iota((NV, SPAN), 1) < NV, ray_t, 0.0)
        ray_ref[step] = dot(eye, first, nt=True, precision=HIGHEST)

    f1[t] = sums
    wait_f1 = offer(f1, t, tiles)
    res_ref[...] = residual
    wait_f1()
    f2[core, chip] = add_up(f1, TILE)
    offer(f2.at[core], chip, chips)()
    hand(f2.at[core], f2.at[core])()
    total = jnp.zeros((NV, SPAN), F32)
    for i in range(CHIPS):
        for c in range(CORES):
            total = total + f2[c, i]
    pv, pp = section_of(total, 0), section_of(total, 1)
    pv_spread = spread(pv, mask)
    gram = pp - dot(pv, pv_spread, nt=True, precision=HIGHEST)
    inverse_spread = spread(inverse_factor(gram), mask)
    block = block - dot(pv_spread[:ROWS, :ROWS], basis, precision=HIGHEST)
    basis_ref[...] = dot(inverse_spread[:ROWS, :ROWS], block, precision=HIGHEST)

    for ref, index in used:
        await_bytes(ref, send, index)


def hand_out(ray, basis, residual, ray_out, basis_out, residual_out):
    basis_out[...] = basis[...]
    residual_out[...] = residual[...]
    ray_out[...] = ray[...]


def per_device(coeff, energy, ranks, assign, screen, initial):
    width = initial.shape[2]
    count = initial.shape[0] * GRP * width * TILE
    vmem = pl.BlockSpec(memory_space=pltpu.VMEM)
    hbm = pl.BlockSpec(memory_space=pltpu.HBM)
    ray, basis, residual = pl.pallas_call(
        functools.partial(body, count),
        out_shape=[
            jax.ShapeDtypeStruct((ITERS, NV, NV), F32),
            jax.ShapeDtypeStruct((ROWS, width), F32),
            jax.ShapeDtypeStruct((ROWS, width), F32),
        ],
        in_specs=[hbm] * 6,
        out_specs=[vmem, vmem, vmem],
        scratch_shapes=[
            pltpu.VMEM(coeff.shape, BF16),
            pltpu.VMEM(screen.shape, BF16),
            pltpu.VMEM((ITERS, TILE, NV, SPAN), F32),
            pltpu.VMEM((ITERS, CORES, CHIPS, NV, SPAN), F32),
            pltpu.VMEM((ITERS, TILE, ROWS, LEV), F32),
            pltpu.VMEM((ITERS, CORES, CHIPS, ROWS, LEV), F32),
            pltpu.VMEM((ALL, LEV), F32),
            pltpu.VMEM((ALL, LEV), BF16),
            pltpu.VMEM((ALL // 2, LEV), F32),
            pltpu.VMEM((ALL, ALL // 2), BF16),
            pltpu.VMEM((ALL // 2, ALL), BF16),
            pltpu.VMEM((ALL // 2, LEV), F32),
            pltpu.VMEM((ITERS, ALL // 2, LEV), BF16),
            pltpu.VMEM((ITERS, ALL // 2, LEV), BF16),
            pltpu.VMEM((ITERS, NV, SPAN), F32),
            pltpu.VMEM((ITERS, NV, SPAN), F32),
            pltpu.VMEM((ITERS, CHIPS, ROWS, LEV), BF16),
            pltpu.VMEM((ITERS, CHIPS, ROWS, LEV), BF16),
            pltpu.VMEM((ITERS, CHIPS, NV, SPAN), F32),
            pltpu.VMEM((ITERS, TILE, ROWS, LEV), BF16),
            pltpu.VMEM((ITERS, TILE, NV, SPAN), F32),
            pltpu.VMEM((TILE, NV, SPAN), F32),
            pltpu.VMEM((CORES, CHIPS, NV, SPAN), F32),
            pltpu.SMEM(assign.shape, jnp.int32),
            pltpu.VMEM(ranks.shape, jnp.int32),
            pltpu.VMEM(energy.shape, F32),
            pltpu.VMEM((ROWS, width), F32),
            pltpu.SemaphoreType.DMA((6,)),
            pltpu.SemaphoreType.DMA((SEMS,)),
            pltpu.SemaphoreType.DMA((SEMS,)),
        ],
        compiler_params=pltpu.CompilerParams(
            collective_id=0, has_side_effects=True, vmem_limit_bytes=32 * 2**20
        ),
        name="davidson",
    )(*[pltpu.with_memory_space_constraint(a, pltpu.HBM) for a in (assign, ranks, coeff, screen, energy, initial.reshape(ROWS, width))])
    basis, residual = basis.reshape(initial.shape), residual.reshape(initial.shape)
    results = (ray, basis, residual)
    return tuple(pl.pallas_call(
        hand_out,
        out_shape=[jax.ShapeDtypeStruct(r.shape, r.dtype) for r in results],
        in_specs=[vmem] * 3,
        out_specs=[vmem] * 3,
        compiler_params=pltpu.CompilerParams(vmem_limit_bytes=8 * 2**20),
        name="hand_out",
    )(*results))


def solution(mesh):
    placed = (
        P("grp", None, "tile"),
        P("grp", "tile"),
        P(),
        P(("grp", "tile")),
        P(("grp", "tile"), None, None),
        P("grp", None, "tile"),
    )
    return jax.shard_map(
        per_device,
        mesh=mesh,
        in_specs=placed,
        out_specs=(P(), P("grp", None, "tile"), P("grp", None, "tile")),
        check_vma=False,
    )
```

time: 83.3 us -> 74.1 us (0.89)
  Pallas kernels: 78.2 us -> 73.4 us
  local copies, waits for them, and re-layouts: 4.24 us -> 0 us
    pallas_call x1, Pallas kernels: 78.2 us -> 72.7 us  [per_device(): pl.pallas_call(functools.partial(body, count), out_shape=[jax.ShapeDtypeS...]
    unnamed x3 -> x0, local copies, waits for them, and re-layouts: 4.24 us -> none
where the time goes in v3:
time: 74.1 us; the launch traced here: 74 us
  Pallas kernels  73.4 us (99%)
    pallas_call x1, Pallas kernels, per_device(): pl.pallas_call(functools.partial(body, count), out_shape=[jax.ShapeDtypeS...  72.7 us

profile of v3, /device:TPU:1, one launch (start us, length us, event | category | flops | bytes accessed | tf_op | source)
XLA Modules:
  0.0 74.0 jit_solution(9856129975586872831)
XLA Ops:
  0.6 72.7 %davidson.1 = (f32[2,8,8]{2,1,0:T(8,128)S(1)}, f32[32,512]{1,0:T(8,128)S(1)}, f32[32,512]{1,0:T(8,128)S(1)}) custom-call(s32[32]{0:T(128)} %assign_hbm.1, s32[64,64]{1,0:T(8,128)} %ranks_hbm.1, bf16[4,256,512]{2,1,0:T(8,128)(2,1)} %coeff_hbm.1, bf16[32,256,256]{2,1,0:T(8,128)(2,1)} %screen_hbm.1, f32[4,512]{1,0:T(4,128)} %energy_hbm.1, f32[32,512]{1,0:T(8,128)} %bitcast.5), custom_call_target="tpu_custom_call" | custom-call | tf_op jit(solution)/shard_map/davidson/pallas_call | solution.py:377
  73.3 0.7 hand_out.1

commit v4 on v3

--- a/solution.py
+++ b/solution.py
@@ -61,25 +61,52 @@
     return jnp.where(mask, jnp.concatenate([small] * (SPAN // NV), axis=0), 0.0)
 
 
-def inverse_factor(gram):
-    sub, lane = iota((NV, SPAN), 0), iota((NV, SPAN), 1) % NV
-    right = (sub == lane).astype(F32)
-    pivots = jnp.ones((NV, SPAN), F32)
+def factor(gram, ridge=False):
+    whole = (NV, SPAN)
+    columns = [jnp.broadcast_to(gram[:, m:m + 1], whole) for m in range(NV)]
+    e = [[jnp.broadcast_to(columns[m][n:n + 1, :], whole) for m in range(n + 1)] for n in range(NV)]
+    if ridge:
+        trace = e[0][0]
+        for n in range(1, NV):
+            trace = trace + e[n][n]
+        for n in range(NV):
+            e[n][n] = e[n][n] + (trace * 1e-6 + 1e-30)
+    unit = [[None] * NV for _ in range(NV)]
     for j in range(NV):
-        row, other = gram[j:j + 1, :], right[j:j + 1, :]
-        pivot = jnp.broadcast_to(row[:, j:j + 1], (NV, SPAN))
-        pivots = jnp.where(sub == j, pivot, pivots)
-        factor = jnp.broadcast_to(gram[:, j:j + 1], (NV, SPAN)) / pivot
-        factor = jnp.where(sub > j, factor, 0.0)
-        gram = gram - factor * row
-        right = right - factor * other
-    return right * lax.rsqrt(pivots)
+        inverse_pivot = 1.0 / e[j][j]
+        for i in range(j + 1, NV):
+            unit[i][j] = e[i][j] * inverse_pivot
+            for m in range(j + 1, i + 1):
+                e[i][m] = e[i][m] - unit[i][j] * e[m][j]
+    back = [[None] * NV for _ in range(NV)]
+    for j in range(NV):
+        for i in range(j + 1, NV):
+            value = unit[i][j]
+            for q in range(j + 1, i):
+                value = value + unit[i][q] * back[q][j]
+            back[i][j] = -value
+    scale = [lax.rsqrt(e[n][n]) for n in range(NV)]
+    root = [e[n][n] * scale[n] for n in range(NV)]
+    sub, lane = iota(whole, 0), iota(whole, 1) % NV
+
+    def assemble(entry):
+        out = jnp.zeros(whole, F32)
+        for i in range(NV):
+            row = jnp.zeros(whole, F32)
+            for j in range(i + 1):
+                row = jnp.where(lane == j, entry(i, j), row)
+            out = jnp.where(sub == i, row, out)
+        return out
+
+    inverse = assemble(lambda i, j: scale[i] if i == j else scale[i] * back[i][j])
+    lower = assemble(lambda i, j: root[i] if i == j else unit[i][j] * root[j])
+    return inverse, lower
 
 
 def body(
     count, assign_hbm, ranks_hbm, coeff_hbm, screen_hbm, energy_hbm, x_hbm,
     ray_ref, basis_ref, res_ref,
-    coeff, screen, g1, g2, d1, d2, dens, dens_b, term, e8, pick, keep,
+    coeff, screen, g1, g2, t2, d1, d2, dens, dens_b, term, e8, pick, keep,
     r1s, r1, a1s, a1, r2s, r2, a2, r3, a3, f1, f2,
     assign_ref, ranks_ref, energy_ref, x_ref, load_sem, send, recv,
 ):
@@ -150,13 +177,13 @@
         full = jnp.where(mask_gram, dot(left, right, nt=True, precision=HIGHEST), 0.0)
         return jnp.concatenate([sum_groups(full[:ROWS]), sum_groups(full[ROWS:])], axis=1)
 
-    def project(block):
+    def by_k_point(block, nt):
         low = block - block.astype(BF16).astype(F32)
         out = []
         for k in range(LK):
             rows = slice(k * NV, (k + 1) * NV)
             both = jnp.concatenate([block[rows], low[rows]], axis=0).astype(BF16)
-            got = dot(both, coeff[k], nt=True)
+            got = dot(both, coeff[k], nt=nt)
             out.append(got[:NV] + got[NV:])
         return jnp.concatenate(out, axis=0)
 
@@ -210,7 +237,7 @@
     zeros = jnp.zeros_like(block)
     sums = grams(jnp.concatenate([block, energy * block], 0), jnp.concatenate([zeros, block], 0))
     loads[2].wait()
-    payload = project(block)
+    payload = by_k_point(block, True)
     pl.semaphore_wait(barrier, len(peers))
 
     basis = None
@@ -222,16 +249,22 @@
         g1[step, t] = sums
         wait_g1 = offer(g1.at[step], t, tiles)
         if step:
-            payload = project(block)
+            payload = by_k_point(block, True)
         d1[step, t] = payload
         wait_d1 = offer(d1.at[step], t, tiles)
         if step == 0:
             one_hots()
         wait_g1()
-        g2[step, core, chip] = add_up(g1.at[step], TILE)
+        total = add_up(g1.at[step], TILE)
+        g2[step, core, chip] = total
         wait_g2 = offer(g2.at[step, core], chip, chips)
+        own_inverse, own_factor = factor(section_of(total, 1), ridge=True)
+        t2[step, core, chip] = own_factor
+        wait_t2 = offer(t2.at[step, core], chip, chips)
+        own_inverse = spread(own_inverse, mask)[:ROWS, :ROWS]
         wait_d1()
-        d2[step, core, chip] = add_up(d1.at[step], TILE)
+        total = add_up(d1.at[step], TILE)
+        d2[step, core, chip] = dot(own_inverse, total, precision=HIGHEST).astype(BF16)
         mine_now = d2.at[step, core, chip]
         arrivals = [next(numbers) for _ in chips]
         for index, device in zip(arrivals, chips):
@@ -240,21 +273,39 @@
         pass_on = next(numbers)
         push(mine_now, mine_now, pass_on, sibling)
         wait_g2()
-        hand(g2.at[step, core], g2.at[step, core])()
-
+        wait_h2 = hand(g2.at[step, core], g2.at[step, core])
+        wait_t2()
+        wait_u2 = hand(t2.at[step, core], t2.at[step, core])
+        wait_h2()
         total = jnp.zeros((NV, SPAN), F32)
         for i in range(CHIPS):
             for c in range(CORES):
                 total = total + g2[step, c, i]
-        pv, pp, rv, rp = [section_of(total, i) for i in range(4)]
+        pv, pp = section_of(total, 0), section_of(total, 1)
         pv_spread = spread(pv, mask)
         gram = pp
         if step:
             gram = pp - dot(pv, pv_spread, nt=True, precision=HIGHEST)
-        inverse = inverse_factor(gram)
+        inverse, _ = factor(gram)
         inverse_spread = spread(inverse, mask)
-        inv_high, inv_low = split(inverse_spread)
-        pv_high, pv_low = split(pv_spread)
+        wait_u2()
+        columns = [jnp.broadcast_to(inverse[:, m:m + 1], (NV, SPAN)) for m in range(NV)]
+        mixers = []
+        for j in range(ALL // SPAN):
+            parts = []
+            for i in range(4):
+                theirs_t = t2[step, j // 2, (j % 2) * 4 + i]
+                mixed = columns[0] * theirs_t[0:1, :]
+                for m in range(1, NV):
+                    mixed = mixed + columns[m] * theirs_t[m:m + 1, :]
+                parts += [mixed] * LK
+            mixers.append(split(jnp.where(mask, jnp.concatenate(parts, axis=0), 0.0)))
+        if step:
+            old = dot(inverse, pv_spread, precision=HIGHEST)
+            old_high, old_low = split(spread(old, mask))
+            for j in range(ALL // SPAN):
+                rows = slice(j * SPAN, (j + 1) * SPAN)
+                dens[rows, :] = apply(old_high, old_low, dens[rows, :])
 
         for index, source in reversed(list(zip(arrivals, from_ids))):
             landed = d2.at[step, core, source]
@@ -265,15 +316,15 @@
         await_bytes(whole, recv, pass_on)
         for j in range(ALL // SPAN):
             rows = slice(j * SPAN, (j + 1) * SPAN)
-            raw = jnp.concatenate(
+            landed = jnp.concatenate(
                 [d2[step, j // 2, (j % 2) * 4 + i] for i in range(4)], axis=0
             )
+            mixed = dot(mixers[j][0], landed) + dot(mixers[j][1], landed)
             if step:
-                raw = raw - apply(pv_high, pv_low, dens[rows, :])
-            raw = apply(inv_high, inv_low, raw)
-            dens_b[rows, :] = raw.astype(BF16)
+                mixed = mixed - dens[rows, :]
+            dens_b[rows, :] = mixed.astype(BF16)
             if step + 1 < ITERS:
-                dens[rows, :] = raw
+                dens[rows, :] = mixed
 
         if step == 0:
             loads[5].wait()
@@ -309,6 +360,7 @@
         a2[step, chip] = coupled + a1[step]
         wait_a2 = offer(a2.at[step], chip, chips)
 
+        rv, rp = section_of(total, 2), section_of(total, 3)
         if step:
             block = block - dot(pv_spread[:ROWS, :ROWS], basis, precision=HIGHEST)
             crossed = dot(rv, pv_spread, nt=True, precision=HIGHEST)
@@ -326,10 +378,7 @@
         a3[step, t] = add_up(a2.at[step], CHIPS)
         wait_a3 = offer(a3.at[step], t, tiles)
         wait_r3()
-        rows_b = add_up(r3.at[step], TILE).astype(BF16)
-        sigma = energy * basis + jnp.concatenate(
-            [dot(rows_b[k * NV:(k + 1) * NV], coeff[k]) for k in range(LK)], axis=0
-        )
+        sigma = energy * basis + by_k_point(add_up(r3.at[step], TILE), False)
         wait_a3()
         ray_t = fold(add_up(a3.at[step], TILE)) * (1.0 / count) + own_energy
         residual = sigma - dot(spread(ray_t, mask)[:ROWS, :ROWS], basis, precision=HIGHEST)
@@ -355,7 +404,7 @@
     pv, pp = section_of(total, 0), section_of(total, 1)
     pv_spread = spread(pv, mask)
     gram = pp - dot(pv, pv_spread, nt=True, precision=HIGHEST)
-    inverse_spread = spread(inverse_factor(gram), mask)
+    inverse_spread = spread(factor(gram)[0], mask)
     block = block - dot(pv_spread[:ROWS, :ROWS], basis, precision=HIGHEST)
     basis_ref[...] = dot(inverse_spread[:ROWS, :ROWS], block, precision=HIGHEST)
 
@@ -388,8 +437,9 @@
             pltpu.VMEM(screen.shape, BF16),
             pltpu.VMEM((ITERS, TILE, NV, SPAN), F32),
             pltpu.VMEM((ITERS, CORES, CHIPS, NV, SPAN), F32),
+            pltpu.VMEM((ITERS, CORES, CHIPS, NV, SPAN), F32),
             pltpu.VMEM((ITERS, TILE, ROWS, LEV), F32),
-            pltpu.VMEM((ITERS, CORES, CHIPS, ROWS, LEV), F32),
+            pltpu.VMEM((ITERS, CORES, CHIPS, ROWS, LEV), BF16),
             pltpu.VMEM((ALL, LEV), F32),
             pltpu.VMEM((ALL, LEV), BF16),
             pltpu.VMEM((ALL // 2, LEV), F32),

time: 74.1 us -> 72.2 us (0.974)
  Pallas kernels: 73.4 us -> 71.5 us
    pallas_call x1, Pallas kernels: 72.7 us -> 70.8 us  [per_device(): pl.pallas_call(functools.partial(body, count), out_shape=[jax.ShapeDtypeS...]
where the time goes in v4:
time: 72.2 us; the launch traced here: 72.1 us
  Pallas kernels  71.5 us (99%)
    pallas_call x1, Pallas kernels, per_device(): pl.pallas_call(functools.partial(body, count), out_shape=[jax.ShapeDtypeS...  70.8 us

profile of v4, /device:TPU:1, one launch (start us, length us, event | category | flops | bytes accessed | tf_op | source)
XLA Modules:
  0.0 72.1 jit_solution(1467828973132688028)
XLA Ops:
  0.6 70.8 %davidson.1 = (f32[2,8,8]{2,1,0:T(8,128)S(1)}, f32[32,512]{1,0:T(8,128)S(1)}, f32[32,512]{1,0:T(8,128)S(1)}) custom-call(s32[32]{0:T(128)} %assign_hbm.1, s32[64,64]{1,0:T(8,128)} %ranks_hbm.1, bf16[4,256,512]{2,1,0:T(8,128)(2,1)} %coeff_hbm.1, bf16[32,256,256]{2,1,0:T(8,128)(2,1)} %screen_hbm.1, f32[4,512]{1,0:T(4,128)} %energy_hbm.1, f32[32,512]{1,0:T(8,128)} %bitcast.5), custom_call_target="tpu_custom_call" | custom-call | tf_op jit(solution)/shard_map/davidson/pallas_call | solution.py:426
  71.5 0.7 hand_out.1

commit v5 on v4

--- a/solution.py
+++ b/solution.py
@@ -106,7 +106,7 @@
 def body(
     count, assign_hbm, ranks_hbm, coeff_hbm, screen_hbm, energy_hbm, x_hbm,
     ray_ref, basis_ref, res_ref,
-    coeff, screen, g1, g2, t2, d1, d2, dens, dens_b, term, e8, pick, keep,
+    coeff, screen, g1, g2, t2, d1, d2, dens, dens_b, term, before, e8, pick, pick_group, keep,
     r1s, r1, a1s, a1, r2s, r2, a2, r3, a3, f1, f2,
     assign_ref, ranks_ref, energy_ref, x_ref, load_sem, send, recv,
 ):
@@ -213,6 +213,8 @@
             pick[:, j * SPAN:(j + 1) * SPAN] = (
                 (lane + j * SPAN == source_row).astype(F32).astype(BF16)
             )
+        group_row = (place(task_col) // ROWS) * NV + iota((half_rows, SPAN), 0) % NV
+        pick_group[...] = (lane == group_row).astype(F32).astype(BF16)
         k_points = GRP * LK
         chosen = dot((lane[:, :k_points] == task_row[:, :k_points]).astype(F32).astype(BF16),
                      ranks_ref[...].astype(F32).astype(BF16))
@@ -276,7 +278,22 @@
         wait_h2 = hand(g2.at[step, core], g2.at[step, core])
         wait_t2()
         wait_u2 = hand(t2.at[step, core], t2.at[step, core])
+        for index, source in reversed(list(zip(arrivals, from_ids))):
+            landed = d2.at[step, core, source]
+            await_bytes(landed, recv, index)
+            push(landed, landed, pass_on, sibling)
         wait_h2()
+        wait_u2()
+        whole = d2.at[step, 0]
+        used.append((whole, pass_on))
+        await_bytes(whole, recv, pass_on)
+        if step == 0:
+            loads[5].wait()
+        chosen = dot(pick[...], d2[step].reshape(ALL, LEV)) * keep[...]
+        for i in range(TASKS):
+            rows = slice(i * NV, (i + 1) * NV)
+            term[rows, :] = dot(chosen[rows].astype(BF16), screen[i], nt=True)
+
         total = jnp.zeros((NV, SPAN), F32)
         for i in range(CHIPS):
             for c in range(CORES):
@@ -288,54 +305,44 @@
             gram = pp - dot(pv, pv_spread, nt=True, precision=HIGHEST)
         inverse, _ = factor(gram)
         inverse_spread = spread(inverse, mask)
-        wait_u2()
         columns = [jnp.broadcast_to(inverse[:, m:m + 1], (NV, SPAN)) for m in range(NV)]
-        mixers = []
-        for j in range(ALL // SPAN):
-            parts = []
-            for i in range(4):
-                theirs_t = t2[step, j // 2, (j % 2) * 4 + i]
-                mixed = columns[0] * theirs_t[0:1, :]
-                for m in range(1, NV):
-                    mixed = mixed + columns[m] * theirs_t[m:m + 1, :]
-                parts += [mixed] * LK
-            mixers.append(split(jnp.where(mask, jnp.concatenate(parts, axis=0), 0.0)))
+        mixed_t = []
+        for j in range(GRP):
+            theirs_t = t2[step, j // CHIPS, j % CHIPS]
+            mixed = columns[0] * theirs_t[0:1, :]
+            for m in range(1, NV):
+                mixed = mixed + columns[m] * theirs_t[m:m + 1, :]
+            mixed_t.append(mixed)
+        group_high, group_low = split(jnp.concatenate(mixed_t, axis=0))
         if step:
             old = dot(inverse, pv_spread, precision=HIGHEST)
             old_high, old_low = split(spread(old, mask))
-            for j in range(ALL // SPAN):
-                rows = slice(j * SPAN, (j + 1) * SPAN)
-                dens[rows, :] = apply(old_high, old_low, dens[rows, :])
-
-        for index, source in reversed(list(zip(arrivals, from_ids))):
-            landed = d2.at[step, core, source]
-            await_bytes(landed, recv, index)
-            push(landed, landed, pass_on, sibling)
-        whole = d2.at[step, 0]
-        used.append((whole, pass_on))
-        await_bytes(whole, recv, pass_on)
+        terms = []
+        for j in range(half_rows // SPAN):
+            rows = slice(j * SPAN, (j + 1) * SPAN)
+            high = jnp.where(mask, dot(pick_group[rows, :], group_high), 0.0).astype(BF16)
+            low = jnp.where(mask, dot(pick_group[rows, :], group_low), 0.0).astype(BF16)
+            result = apply(high, low, term[rows, :])
+            if step:
+                result = result - apply(old_high, old_low, before[rows, :])
+            if step + 1 < ITERS:
+                before[rows, :] = result
+            terms.append(result)
+        term_high, term_low = split(jnp.concatenate(terms, axis=0) * keep[...])
+
+        r1s[step] = (dot(e8[theirs, :], term_high) + dot(e8[theirs, :], term_low)).astype(BF16)
+        wait_r1 = hand(r1s.at[step], r1.at[step])
         for j in range(ALL // SPAN):
             rows = slice(j * SPAN, (j + 1) * SPAN)
-            landed = jnp.concatenate(
-                [d2[step, j // 2, (j % 2) * 4 + i] for i in range(4)], axis=0
-            )
-            mixed = dot(mixers[j][0], landed) + dot(mixers[j][1], landed)
+            parts = [mixed_t[j * 4 + i] for i in range(4) for _ in range(LK)]
+            high, low = split(jnp.where(mask, jnp.concatenate(parts, axis=0), 0.0))
+            landed = d2[step, j // 2, (j % 2) * 4:(j % 2) * 4 + 4].reshape(SPAN, LEV)
+            mixed = dot(high, landed) + dot(low, landed)
             if step:
-                mixed = mixed - dens[rows, :]
+                mixed = mixed - apply(old_high, old_low, dens[rows, :])
             dens_b[rows, :] = mixed.astype(BF16)
             if step + 1 < ITERS:
                 dens[rows, :] = mixed
-
-        if step == 0:
-            loads[5].wait()
-        chosen = dot(pick[...], dens_b[...]) * keep[...]
-        for i in range(TASKS):
-            rows = slice(i * NV, (i + 1) * NV)
-            term[rows, :] = dot(chosen[rows].astype(BF16), screen[i], nt=True)
-        term_high, term_low = split(term[...] * keep[...])
-
-        r1s[step] = (dot(e8[theirs, :], term_high) + dot(e8[theirs, :], term_low)).astype(BF16)
-        wait_r1 = hand(r1s.at[step], r1.at[step])
         own = dot(e8[mine, :], term_high) + dot(e8[mine, :], term_low)
         own_b = own.astype(BF16)
         coupled = jnp.zeros((SPAN, SPAN), F32)
@@ -443,8 +450,10 @@
             pltpu.VMEM((ALL, LEV), F32),
             pltpu.VMEM((ALL, LEV), BF16),
             pltpu.VMEM((ALL // 2, LEV), F32),
+            pltpu.VMEM((ALL // 2, LEV), F32),
             pltpu.VMEM((ALL, ALL // 2), BF16),
             pltpu.VMEM((ALL // 2, ALL), BF16),
+            pltpu.VMEM((ALL // 2, SPAN), BF16),
             pltpu.VMEM((ALL // 2, LEV), F32),
             pltpu.VMEM((ITERS, ALL // 2, LEV), BF16),
             pltpu.VMEM((ITERS, ALL // 2, LEV), BF16),

time: 72.2 us -> 71.3 us (0.988)
  Pallas kernels: 71.5 us -> 70.5 us
    pallas_call x1, Pallas kernels: 70.8 us -> 69.9 us  [per_device(): pl.pallas_call(functools.partial(body, count), out_shape=[jax.ShapeDtypeS...]
where the time goes in v5:
time: 71.3 us; the launch traced here: 71.2 us
  Pallas kernels  70.5 us (99%)
    pallas_call x1, Pallas kernels, per_device(): pl.pallas_call(functools.partial(body, count), out_shape=[jax.ShapeDtypeS...  69.9 us

profile of v5, /device:TPU:1, one launch (start us, length us, event | category | flops | bytes accessed | tf_op | source)
XLA Modules:
  0.0 71.2 jit_solution(6666286730227646895)
XLA Ops:
  0.6 69.9 %davidson.1 = (f32[2,8,8]{2,1,0:T(8,128)S(1)}, f32[32,512]{1,0:T(8,128)S(1)}, f32[32,512]{1,0:T(8,128)S(1)}) custom-call(s32[32]{0:T(128)} %assign_hbm.1, s32[64,64]{1,0:T(8,128)} %ranks_hbm.1, bf16[4,256,512]{2,1,0:T(8,128)(2,1)} %coeff_hbm.1, bf16[32,256,256]{2,1,0:T(8,128)(2,1)} %screen_hbm.1, f32[4,512]{1,0:T(4,128)} %energy_hbm.1, f32[32,512]{1,0:T(8,128)} %bitcast.5), custom_call_target="tpu_custom_call" | custom-call | tf_op jit(solution)/shard_map/davidson/pallas_call | solution.py:433
  70.5 0.7 hand_out.1

commit v6 on v5

--- a/solution.py
+++ b/solution.py
@@ -397,18 +397,36 @@
         first = jnp.where(iota((NV, SPAN), 1) < NV, ray_t, 0.0)
         ray_ref[step] = dot(eye, first, nt=True, precision=HIGHEST)
 
-    f1[t] = sums
-    wait_f1 = offer(f1, t, tiles)
+    group, sub = iota((NV, SPAN), 1) // NV, iota((NV, SPAN), 0)
+    row = jnp.where(group == sub, section_of(sums, 0), 0.0)
+    row = jnp.where(group == sub + NV, section_of(sums, 1), row)
+    row = jnp.sum(row, axis=0, keepdims=True)
+    f1[0] = row
+    hand(f1.at[0], f1.at[1])()
+    y = y_hi * 2 + y_lo
+    slot = (y * 4 + x) * 4 + z
+    f2[slot] = row + f1[1]
+    index = next(numbers)
+    steps = [(a, b, c) for a in range(4) for b in range(4) for c in range(4)]
+    steps.sort(key=lambda o: -sum(min(i, 4 - i) for i in o))
+    for a, b, c in steps[:-1]:
+        to_y = lax.rem(y + a, 4)
+        device = (
+            (lax.rem(to_y, 2) * 4 + lax.rem(x + b, 4)) * CORES + core,
+            lax.div(to_y, 2) * 4 + lax.rem(z + c, 4),
+        )
+        push(f2.at[slot], f2.at[slot], index, device)
     res_ref[...] = residual
-    wait_f1()
-    f2[core, chip] = add_up(f1, TILE)
-    offer(f2.at[core], chip, chips)()
-    hand(f2.at[core], f2.at[core])()
-    total = jnp.zeros((NV, SPAN), F32)
-    for i in range(CHIPS):
-        for c in range(CORES):
-            total = total + f2[c, i]
-    pv, pp = section_of(total, 0), section_of(total, 1)
+    for ref, sent in used:
+        await_bytes(ref, send, sent)
+    used = [(f2.at[pl.ds(0, len(steps) - 1)], index)]
+    await_bytes(used[0][0], recv, index)
+    total = f2[0]
+    for i in range(1, len(steps)):
+        total = total + f2[i]
+    total = jnp.broadcast_to(total, (NV, SPAN))
+    pv = fold(jnp.where(group == sub, total, 0.0))
+    pp = fold(jnp.where(group == sub + NV, total, 0.0))
     pv_spread = spread(pv, mask)
     gram = pp - dot(pv, pv_spread, nt=True, precision=HIGHEST)
     inverse_spread = spread(factor(gram)[0], mask)
@@ -464,8 +482,8 @@
             pltpu.VMEM((ITERS, CHIPS, NV, SPAN), F32),
             pltpu.VMEM((ITERS, TILE, ROWS, LEV), BF16),
             pltpu.VMEM((ITERS, TILE, NV, SPAN), F32),
-            pltpu.VMEM((TILE, NV, SPAN), F32),
-            pltpu.VMEM((CORES, CHIPS, NV, SPAN), F32),
+            pltpu.VMEM((CORES, 1, SPAN), F32),
+            pltpu.VMEM((CHIPS * TILE, 1, SPAN), F32),
             pltpu.SMEM(assign.shape, jnp.int32),
             pltpu.VMEM(ranks.shape, jnp.int32),
             pltpu.VMEM(energy.shape, F32),

time: 71.3 us -> 68.2 us (0.957)
  Pallas kernels: 70.5 us -> 67.4 us
    pallas_call x1, Pallas kernels: 69.9 us -> 66.8 us  [per_device(): pl.pallas_call(functools.partial(body, count), out_shape=[jax.ShapeDtypeS...]
where the time goes in v6:
time: 68.2 us; the launch traced here: 68.1 us
  Pallas kernels  67.4 us (99%)
    pallas_call x1, Pallas kernels, per_device(): pl.pallas_call(functools.partial(body, count), out_shape=[jax.ShapeDtypeS...  66.8 us

profile of v6, /device:TPU:1, one launch (start us, length us, event | category | flops | bytes accessed | tf_op | source)
XLA Modules:
  0.0 68.1 jit_solution(570747462642757404)
XLA Ops:
  0.6 66.8 %davidson.1 = (f32[2,8,8]{2,1,0:T(8,128)S(1)}, f32[32,512]{1,0:T(8,128)S(1)}, f32[32,512]{1,0:T(8,128)S(1)}) custom-call(s32[32]{0:T(128)} %assign_hbm.1, s32[64,64]{1,0:T(8,128)} %ranks_hbm.1, bf16[4,256,512]{2,1,0:T(8,128)(2,1)} %coeff_hbm.1, bf16[32,256,256]{2,1,0:T(8,128)(2,1)} %screen_hbm.1, f32[4,512]{1,0:T(4,128)} %energy_hbm.1, f32[32,512]{1,0:T(8,128)} %bitcast.5), custom_call_target="tpu_custom_call" | custom-call | tf_op jit(solution)/shard_map/davidson/pallas_call | solution.py:451
  67.4 0.7 hand_out.1

commit v7 on v6

--- a/solution.py
+++ b/solution.py
@@ -34,6 +34,14 @@
 def split(a):
     high = a.astype(BF16)
     return high, (a - high.astype(F32)).astype(BF16)
+
+
+def dot3(a, b, nt=False):
+    rows = a.shape[0]
+    high, low = split(b)
+    both = jnp.concatenate([a, a - a.astype(BF16).astype(F32)], axis=0).astype(BF16)
+    first = dot(both, high, nt=nt)
+    return first[:rows] + (first[rows:] + dot(both[:rows], low, nt=nt))
 
 
 def iota(shape, dim):
@@ -174,8 +182,13 @@
     section = iota((NV, SPAN), 1) // ROWS
 
     def grams(left, right):
-        full = jnp.where(mask_gram, dot(left, right, nt=True, precision=HIGHEST), 0.0)
+        full = jnp.where(mask_gram, dot3(left, right, nt=True), 0.0)
         return jnp.concatenate([sum_groups(full[:ROWS]), sum_groups(full[ROWS:])], axis=1)
+
+    def store_ray(step):
+        eye = (iota((NV, SPAN), 0) == iota((NV, SPAN), 1)).astype(F32)
+        first = jnp.where(iota((NV, SPAN), 1) < NV, ray_t, 0.0)
+        ray_ref[step] = dot(eye, first, nt=True, precision=HIGHEST)
 
     def by_k_point(block, nt):
         low = block - block.astype(BF16).astype(F32)
@@ -256,6 +269,8 @@
         wait_d1 = offer(d1.at[step], t, tiles)
         if step == 0:
             one_hots()
+        else:
+            store_ray(step - 1)
         wait_g1()
         total = add_up(g1.at[step], TILE)
         g2[step, core, chip] = total
@@ -266,7 +281,7 @@
         own_inverse = spread(own_inverse, mask)[:ROWS, :ROWS]
         wait_d1()
         total = add_up(d1.at[step], TILE)
-        d2[step, core, chip] = dot(own_inverse, total, precision=HIGHEST).astype(BF16)
+        d2[step, core, chip] = dot3(own_inverse, total).astype(BF16)
         mine_now = d2.at[step, core, chip]
         arrivals = [next(numbers) for _ in chips]
         for index, device in zip(arrivals, chips):
@@ -302,7 +317,7 @@
         pv_spread = spread(pv, mask)
         gram = pp
         if step:
-            gram = pp - dot(pv, pv_spread, nt=True, precision=HIGHEST)
+            gram = pp - dot3(pv, pv_spread, nt=True)
         inverse, _ = factor(gram)
         inverse_spread = spread(inverse, mask)
         columns = [jnp.broadcast_to(inverse[:, m:m + 1], (NV, SPAN)) for m in range(NV)]
@@ -315,7 +330,7 @@
             mixed_t.append(mixed)
         group_high, group_low = split(jnp.concatenate(mixed_t, axis=0))
         if step:
-            old = dot(inverse, pv_spread, precision=HIGHEST)
+            old = dot3(inverse, pv_spread)
             old_high, old_low = split(spread(old, mask))
         terms = []
         for j in range(half_rows // SPAN):
@@ -369,14 +384,14 @@
 
         rv, rp = section_of(total, 2), section_of(total, 3)
         if step:
-            block = block - dot(pv_spread[:ROWS, :ROWS], basis, precision=HIGHEST)
-            crossed = dot(rv, pv_spread, nt=True, precision=HIGHEST)
-            crossed_t = dot(pv, spread(rv, mask), nt=True, precision=HIGHEST)
-            inner = dot(pv, spread(own_energy, mask), precision=HIGHEST)
-            rp = rp - crossed - crossed_t + dot(inner, pv_spread, nt=True, precision=HIGHEST)
-        basis = dot(inverse_spread[:ROWS, :ROWS], block, precision=HIGHEST)
-        half = dot(inverse, spread(rp, mask), precision=HIGHEST)
-        own_energy = dot(half, inverse_spread, nt=True, precision=HIGHEST)
+            block = block - dot3(pv_spread[:ROWS, :ROWS], basis)
+            crossed = dot3(rv, pv_spread, nt=True)
+            crossed_t = dot3(pv, spread(rv, mask), nt=True)
+            inner = dot3(pv, spread(own_energy, mask))
+            rp = rp - crossed - crossed_t + dot3(inner, pv_spread, nt=True)
+        basis = dot3(inverse_spread[:ROWS, :ROWS], block)
+        half = dot3(inverse, spread(rp, mask))
+        own_energy = dot3(half, inverse_spread, nt=True)
 
         await_bytes(r2_size, recv, r2_index)
         r3[step, t] = add_up(r2.at[step], CHIPS).astype(BF16)
@@ -388,14 +403,11 @@
         sigma = energy * basis + by_k_point(add_up(r3.at[step], TILE), False)
         wait_a3()
         ray_t = fold(add_up(a3.at[step], TILE)) * (1.0 / count) + own_energy
-        residual = sigma - dot(spread(ray_t, mask)[:ROWS, :ROWS], basis, precision=HIGHEST)
+        residual = sigma - dot3(spread(ray_t, mask)[:ROWS, :ROWS], basis)
         block = residual / energy
         sums = grams(
             jnp.concatenate([block, residual], 0), jnp.concatenate([basis, block], 0)
         )
-        eye = (iota((NV, SPAN), 0) == iota((NV, SPAN), 1)).astype(F32)
-        first = jnp.where(iota((NV, SPAN), 1) < NV, ray_t, 0.0)
-        ray_ref[step] = dot(eye, first, nt=True, precision=HIGHEST)
 
     group, sub = iota((NV, SPAN), 1) // NV, iota((NV, SPAN), 0)
     row = jnp.where(group == sub, section_of(sums, 0), 0.0)
@@ -417,6 +429,7 @@
         )
         push(f2.at[slot], f2.at[slot], index, device)
     res_ref[...] = residual
+    store_ray(ITERS - 1)
     for ref, sent in used:
         await_bytes(ref, send, sent)
     used = [(f2.at[pl.ds(0, len(steps) - 1)], index)]
@@ -428,10 +441,10 @@
     pv = fold(jnp.where(group == sub, total, 0.0))
     pp = fold(jnp.where(group == sub + NV, total, 0.0))
     pv_spread = spread(pv, mask)
-    gram = pp - dot(pv, pv_spread, nt=True, precision=HIGHEST)
+    gram = pp - dot3(pv, pv_spread, nt=True)
     inverse_spread = spread(factor(gram)[0], mask)
-    block = block - dot(pv_spread[:ROWS, :ROWS], basis, precision=HIGHEST)
-    basis_ref[...] = dot(inverse_spread[:ROWS, :ROWS], block, precision=HIGHEST)
+    block = block - dot3(pv_spread[:ROWS, :ROWS], basis)
+    basis_ref[...] = dot3(inverse_spread[:ROWS, :ROWS], block)
 
     for ref, index in used:
         await_bytes(ref, send, index)

time: 68.2 us -> 66.8 us (0.979)
  Pallas kernels: 67.4 us -> 66.1 us
    pallas_call x1, Pallas kernels: 66.8 us -> 65.4 us  [per_device(): pl.pallas_call(functools.partial(body, count), out_shape=[jax.ShapeDtypeS...]
where the time goes in v7:
time: 66.8 us; the launch traced here: 66.7 us
  Pallas kernels  66.1 us (99%)
    pallas_call x1, Pallas kernels, per_device(): pl.pallas_call(functools.partial(body, count), out_shape=[jax.ShapeDtypeS...  65.4 us

profile of v7, /device:TPU:1, one launch (start us, length us, event | category | flops | bytes accessed | tf_op | source)
XLA Modules:
  0.0 66.7 jit_solution(10976340788287649357)
XLA Ops:
  0.6 65.4 %davidson.1 = (f32[2,8,8]{2,1,0:T(8,128)S(1)}, f32[32,512]{1,0:T(8,128)S(1)}, f32[32,512]{1,0:T(8,128)S(1)}) custom-call(s32[32]{0:T(128)} %assign_hbm.1, s32[64,64]{1,0:T(8,128)} %ranks_hbm.1, bf16[4,256,512]{2,1,0:T(8,128)(2,1)} %coeff_hbm.1, bf16[32,256,256]{2,1,0:T(8,128)(2,1)} %screen_hbm.1, f32[4,512]{1,0:T(4,128)} %energy_hbm.1, f32[32,512]{1,0:T(8,128)} %bitcast.5), custom_call_target="tpu_custom_call" | custom-call | tf_op jit(solution)/shard_map/davidson/pallas_call | solution.py:464
  66.1 0.7 hand_out.1

commit v8 on v7

--- a/solution.py
+++ b/solution.py
@@ -114,7 +114,7 @@
 def body(
     count, assign_hbm, ranks_hbm, coeff_hbm, screen_hbm, energy_hbm, x_hbm,
     ray_ref, basis_ref, res_ref,
-    coeff, screen, g1, g2, t2, d1, d2, dens, dens_b, term, before, e8, pick, pick_group, keep,
+    coeff, screen, g1, g2, d1, d2, dens, dens_b, term, before, e8, pick, pick_group, keep,
     r1s, r1, a1s, a1, r2s, r2, a2, r3, a3, f1, f2,
     assign_ref, ranks_ref, energy_ref, x_ref, load_sem, send, recv,
 ):
@@ -273,11 +273,10 @@
             store_ray(step - 1)
         wait_g1()
         total = add_up(g1.at[step], TILE)
-        g2[step, core, chip] = total
+        g2[step, core, chip, 0:NV] = total
+        own_inverse, own_factor = factor(section_of(total, 1), ridge=True)
+        g2[step, core, chip, NV:] = own_factor
         wait_g2 = offer(g2.at[step, core], chip, chips)
-        own_inverse, own_factor = factor(section_of(total, 1), ridge=True)
-        t2[step, core, chip] = own_factor
-        wait_t2 = offer(t2.at[step, core], chip, chips)
         own_inverse = spread(own_inverse, mask)[:ROWS, :ROWS]
         wait_d1()
         total = add_up(d1.at[step], TILE)
@@ -291,14 +290,11 @@
         push(mine_now, mine_now, pass_on, sibling)
         wait_g2()
         wait_h2 = hand(g2.at[step, core], g2.at[step, core])
-        wait_t2()
-        wait_u2 = hand(t2.at[step, core], t2.at[step, core])
         for index, source in reversed(list(zip(arrivals, from_ids))):
             landed = d2.at[step, core, source]
             await_bytes(landed, recv, index)
             push(landed, landed, pass_on, sibling)
         wait_h2()
-        wait_u2()
         whole = d2.at[step, 0]
         used.append((whole, pass_on))
         await_bytes(whole, recv, pass_on)
@@ -312,7 +308,7 @@
         total = jnp.zeros((NV, SPAN), F32)
         for i in range(CHIPS):
             for c in range(CORES):
-                total = total + g2[step, c, i]
+                total = total + g2[step, c, i, 0:NV]
         pv, pp = section_of(total, 0), section_of(total, 1)
         pv_spread = spread(pv, mask)
         gram = pp
@@ -323,7 +319,7 @@
         columns = [jnp.broadcast_to(inverse[:, m:m + 1], (NV, SPAN)) for m in range(NV)]
         mixed_t = []
         for j in range(GRP):
-            theirs_t = t2[step, j // CHIPS, j % CHIPS]
+            theirs_t = g2[step, j // CHIPS, j % CHIPS, NV:]
             mixed = columns[0] * theirs_t[0:1, :]
             for m in range(1, NV):
                 mixed = mixed + columns[m] * theirs_t[m:m + 1, :]
@@ -434,9 +430,10 @@
         await_bytes(ref, send, sent)
     used = [(f2.at[pl.ds(0, len(steps) - 1)], index)]
     await_bytes(used[0][0], recv, index)
-    total = f2[0]
-    for i in range(1, len(steps)):
-        total = total + f2[i]
+    totals = [f2[i] for i in range(len(steps))]
+    while len(totals) > 1:
+        totals = [left + right for left, right in zip(totals[::2], totals[1::2])]
+    total = totals[0]
     total = jnp.broadcast_to(total, (NV, SPAN))
     pv = fold(jnp.where(group == sub, total, 0.0))
     pp = fold(jnp.where(group == sub + NV, total, 0.0))
@@ -474,8 +471,7 @@
             pltpu.VMEM(coeff.shape, BF16),
             pltpu.VMEM(screen.shape, BF16),
             pltpu.VMEM((ITERS, TILE, NV, SPAN), F32),
-            pltpu.VMEM((ITERS, CORES, CHIPS, NV, SPAN), F32),
-            pltpu.VMEM((ITERS, CORES, CHIPS, NV, SPAN), F32),
+            pltpu.VMEM((ITERS, CORES, CHIPS, 2 * NV, SPAN), F32),
             pltpu.VMEM((ITERS, TILE, ROWS, LEV), F32),
             pltpu.VMEM((ITERS, CORES, CHIPS, ROWS, LEV), BF16),
             pltpu.VMEM((ALL, LEV), F32),

time: 66.8 us -> 66.8 us (level)
  no operation moved by 1% of the time
where the time goes in v8:
time: 66.8 us; the launch traced here: 66.7 us
  Pallas kernels  66 us (99%)
    pallas_call x1, Pallas kernels, per_device(): pl.pallas_call(functools.partial(body, count), out_shape=[jax.ShapeDtypeS...  65.4 us

profile of v8, /device:TPU:1, one launch (start us, length us, event | category | flops | bytes accessed | tf_op | source)
XLA Modules:
  0.0 66.7 jit_solution(3934160571667147981)
XLA Ops:
  0.6 65.4 %davidson.1 = (f32[2,8,8]{2,1,0:T(8,128)S(1)}, f32[32,512]{1,0:T(8,128)S(1)}, f32[32,512]{1,0:T(8,128)S(1)}) custom-call(s32[32]{0:T(128)} %assign_hbm.1, s32[64,64]{1,0:T(8,128)} %ranks_hbm.1, bf16[4,256,512]{2,1,0:T(8,128)(2,1)} %coeff_hbm.1, bf16[32,256,256]{2,1,0:T(8,128)(2,1)} %screen_hbm.1, f32[4,512]{1,0:T(4,128)} %energy_hbm.1, f32[32,512]{1,0:T(8,128)} %bitcast.5), custom_call_target="tpu_custom_call" | custom-call | tf_op jit(solution)/shard_map/davidson/pallas_call | solution.py:461
  66.0 0.7 hand_out.1
